TPU v7x, 256 devices: a whole 4x4x8 slice. The times are simulated.
256 devices in a mesh: seq: 64 (over x, z, core), head: 4 (over y).
Axes of the slice: x: 4, y: 4, z: 8, core: 2. Of those that a mesh axis runs over, the one named last changes fastest.
Arguments:
- queries: bfloat16 [16384, 4096], P('seq', 'head'), may hold values from -1.796875 to 1.796875
- key_vectors: bfloat16 [16384, 4096], P('seq', 'head'), may hold values from -1.796875 to 1.796875
- values: bfloat16 [16384, 4096], P('seq', 'head'), may hold values from -96 to 96
- decay_log: float32 [32, 16384], P('head', 'seq'), may hold values from -2 to 0
- doc_starts: int32 [64, 4], P('seq'), may hold values from 0 to 256, as said below
- gate_logits: bfloat16 [16384, 4096], P('seq', 'head'), may hold values from -6 to 6
- norm_gain: float32 [4096], P('head'), may hold values from 0.1 to 1.9
- grad_out: bfloat16 [16384, 4096], P('seq', 'head'), may hold values from -6 to 6
Outputs:
- grad_query: bfloat16 [16384, 4096], P('seq', 'head')
- grad_key: bfloat16 [16384, 4096], P('seq', 'head')
- grad_value: bfloat16 [16384, 4096], P('seq', 'head')
- grad_gate: bfloat16 [16384, 4096], P('seq', 'head')
Inputs may be any that keep to these rules, and one draw needn't show every extreme that they name: `doc_starts`: each row lists in rising order the offsets within its shard of 256 tokens at which documents start, then 256 in unused places; some shard has 4 starts, the first at 0, and some shard has none.
All inputs are finite; a program needn't handle non-finite values.
Results may differ from a plain program's by a relative error of at most 0.0057.
Values sent between devices are 32-bit elements; how exact they have to be, the bound alone decides.
No kernel may reach another device: no remote copies, remote signals or barrier semaphores. Data moves between devices by JAX's collectives and lax.ppermute only.
A program may use at most 128 MiB of HBM per device.

v0:
```python
import jax
import jax.numpy as jnp
from jax import lax
from jax.sharding import PartitionSpec as P

HEAD_DIM = 128
BLOCK = 256


highest = lax.Precision.HIGHEST
epsilon = 1e-06


def prefix(part, axis, combine, identity, reverse):
    count = lax.axis_size(axis)
    place = lax.axis_index(axis)
    ahead = count - 1 - place if reverse else place
    gathered = jax.tree.map(lambda a: lax.all_gather(a, axis), part)
    state = jax.tree.map(lambda a, e: jnp.zeros_like(a) + jnp.asarray(e, a.dtype), part, identity)

    def one(turn, state):
        source = count - 1 - turn if reverse else turn
        return combine(
            state, jax.tree.map(lambda a: lax.dynamic_index_in_dim(a, source, 0, False), gathered)
        )

    return lax.fori_loop(0, ahead, one, state)


def block_factors(decay_block, start_block):
    counted = jnp.cumsum(start_block, axis=-1)
    summed = jnp.cumsum(decay_block, axis=-1)
    length = start_block.shape[-1]
    element_slots_along_text = jnp.arange(length)
    causal = element_slots_along_text[:, None] >= element_slots_along_text[None, :]
    keeper = jnp.logical_and(causal[None], counted[:, :, None] == counted[:, None, :])[:, None]
    spread = summed[:, :, :, None] - summed[:, :, None, :]
    multiplier = jnp.where(keeper, jnp.exp(jnp.where(keeper, spread, 0.0)), 0.0)
    inward = jnp.where((counted == 0)[:, None, :], jnp.exp(summed), 0.0)
    latest = counted[:, -1:]
    outward = jnp.where((counted == latest)[:, None, :], jnp.exp(summed[:, :, -1:] - summed), 0.0)
    through = jnp.where(latest == 0, jnp.exp(summed[:, :, -1]), 0.0)
    return (multiplier, inward, outward, through)


def link_states(earlier, later):
    return (earlier[0] * later[0], later[0][:, None, None] * earlier[1] + later[1])


def local_chain(through, sums_here, backward):

    def advance(carried, pieces):
        memory, factor = carried
        rate_here, addition = pieces
        return (
            (rate_here[:, None, None] * memory + addition, factor * rate_here),
            (memory, factor),
        )

    initial = (jnp.zeros_like(sums_here[0]), jnp.ones_like(through[0]))
    closing, before = lax.scan(advance, initial, (through, sums_here), reverse=backward)
    return (closing, before)


def local(queries, key_vectors, values, decay_log, doc_starts, gate_logits, norm_gain, grad_out):
    tok_count = queries.shape[0]
    heads_here = queries.shape[1] // HEAD_DIM
    count_blocks = tok_count // BLOCK
    features = queries.shape[1] * lax.axis_size("head")
    element_slots_along_text = jnp.arange(tok_count, dtype=jnp.int32)
    start_marks = jnp.any(
        doc_starts[0][:, None] == element_slots_along_text[None, :], axis=0
    ).astype(jnp.int32)
    start_marks = start_marks.reshape(count_blocks, BLOCK)
    decays = decay_log.reshape(heads_here, count_blocks, BLOCK).transpose(1, 0, 2)

    def shaped(array):
        return array.reshape(count_blocks, BLOCK, heads_here, HEAD_DIM)

    query_blocks = shaped(queries)
    key_blocks = shaped(key_vectors)
    value_blocks = shaped(values)
    multiplier, inward, outward, through = block_factors(decays, start_marks)
    inward_rows = inward.transpose(0, 2, 1)[..., None]
    outward_rows = outward.transpose(0, 2, 1)[..., None]
    scores = jnp.einsum(
        "nthd,nshd->nhts", query_blocks, key_blocks, preferred_element_type=jnp.float32
    )
    mixing = (multiplier * scores).astype(jnp.bfloat16)
    within = jnp.einsum("nhts,nshd->nthd", mixing, value_blocks, preferred_element_type=jnp.float32)
    key_scaled = (key_blocks.astype(jnp.float32) * outward_rows).astype(jnp.bfloat16)
    sums_here = jnp.einsum(
        "nshd,nshe->nhde", key_scaled, value_blocks, preferred_element_type=jnp.float32
    )
    (summary, through_dev), (starts_local, factors_local) = local_chain(through, sums_here, False)
    _, incoming = prefix(
        (through_dev, summary),
        "seq",
        link_states,
        (jnp.ones_like(through_dev), jnp.zeros_like(summary)),
        False,
    )
    incoming_state = factors_local[:, :, None, None] * incoming[None] + starts_local
    carried = (
        jnp.einsum(
            "nthd,nhde->nthe",
            query_blocks,
            incoming_state,
            precision=highest,
            preferred_element_type=jnp.float32,
        )
        * inward_rows
    )
    attended = (within + carried).reshape(tok_count, queries.shape[1])
    opening = jax.nn.sigmoid(gate_logits.astype(jnp.float32))
    upstream = grad_out.astype(jnp.float32)
    dnormed = upstream * norm_gain[None, :] * opening
    squares = jnp.sum(attended * attended, axis=1)
    totals = lax.psum(squares, "head")
    spread_rms = jnp.sqrt(totals / features + epsilon)
    normed = attended / spread_rms[:, None]
    projection = lax.psum(jnp.sum(dnormed * normed, axis=1), "head") / features
    grad_gate = (upstream * norm_gain[None, :] * normed * opening * (1.0 - opening)).astype(
        jnp.bfloat16
    )
    grad_attn = ((dnormed - normed * projection[:, None]) / spread_rms[:, None]).astype(
        jnp.bfloat16
    )
    grad_blocks = shaped(grad_attn)
    query_scaled = (query_blocks.astype(jnp.float32) * inward_rows).astype(jnp.bfloat16)
    back_sums = jnp.einsum(
        "nthd,nthe->nhde", query_scaled, grad_blocks, preferred_element_type=jnp.float32
    )
    (back_summary, _), (reverse_inner_product, back_factors) = local_chain(through, back_sums, True)
    _, arriving = prefix(
        (through_dev, back_summary),
        "seq",
        link_states,
        (jnp.ones_like(through_dev), jnp.zeros_like(back_summary)),
        True,
    )
    leaving = back_factors[:, :, None, None] * arriving[None] + reverse_inner_product
    scores_gradient = jnp.einsum(
        "nthe,nshe->nhts", grad_blocks, value_blocks, preferred_element_type=jnp.float32
    )
    grad_mixing = (multiplier * scores_gradient).astype(jnp.bfloat16)
    grad_query = jnp.einsum(
        "nhts,nshd->nthd", grad_mixing, key_blocks, preferred_element_type=jnp.float32
    )
    grad_query = (
        grad_query
        + jnp.einsum(
            "nthe,nhde->nthd",
            grad_blocks,
            incoming_state,
            precision=highest,
            preferred_element_type=jnp.float32,
        )
        * inward_rows
    )
    grad_key = jnp.einsum(
        "nhts,nthd->nshd", grad_mixing, query_blocks, preferred_element_type=jnp.float32
    )
    grad_key = (
        grad_key
        + jnp.einsum(
            "nshe,nhde->nshd",
            value_blocks,
            leaving,
            precision=highest,
            preferred_element_type=jnp.float32,
        )
        * outward_rows
    )
    grad_value = jnp.einsum(
        "nhts,nthe->nshe", mixing, grad_blocks, preferred_element_type=jnp.float32
    )
    grad_value = (
        grad_value
        + jnp.einsum(
            "nshd,nhde->nshe",
            key_blocks,
            leaving,
            precision=highest,
            preferred_element_type=jnp.float32,
        )
        * outward_rows
    )
    width = queries.shape[1]
    return (
        grad_query.reshape(tok_count, width).astype(jnp.bfloat16),
        grad_key.reshape(tok_count, width).astype(jnp.bfloat16),
        grad_value.reshape(tok_count, width).astype(jnp.bfloat16),
        grad_gate,
    )


def solution(mesh):
    placed = (
        P("seq", "head"),
        P("seq", "head"),
        P("seq", "head"),
        P("head", "seq"),
        P("seq", None),
        P("seq", "head"),
        P("head"),
        P("seq", "head"),
    )
    return jax.shard_map(
        local,
        mesh=mesh,
        in_specs=placed,
        out_specs=(P("seq", "head"), P("seq", "head"), P("seq", "head"), P("seq", "head")),
        check_vma=False,
    )
```

profile of v0, /device:TPU:1, one launch (start us, length us, event | category | flops | bytes accessed | tf_op | source)
XLA Modules:
  0.0 491.2 jit_solution(1963937035526489559)
XLA Ops:
  7.2 1.3 reduce-window.16
  11.5 1.2 copy.146
  16.2 43.9 %all-gather = f32[64,8,1]{1,2,0:T(1,128)S(1)} all-gather(f32[1,8,1]{1,2,0:T(1,128)S(1)} %copy.115), channel_id=2, replica_groups=mesh['seq'=64,'head'=4] {'seq'}, dimensions={0}, use_global_device_ids=true | all-gather | bytes 2080 | tf_op jit(solution)/shard_map/all_gather | solution.py:18
  62.6 99.7 %all-gather.6.cloned.1.call-done = f32[512,128,128]{2,1,0:T(8,128)} async-done(((f32[8,128,128]{2,1,0:T(8,128)}), f32[512,128,128]{2,1,0:T(8,128)}) %all-gather.6.cloned.1.call-update) | async-done | bytes 33554448 | tf_op jit(solution)/shard_map/all_gather | solution.py:18
  162.3 1.2 while.16
  162.3 1.2 bitcast_add_fusion.9
  163.5 1.7 multiply_reduce_fusion.1
  165.2 1.6 copy.122
  166.8 8.5 %psum.14 = f32[256]{0:T(256)S(1)} all-reduce(f32[256]{0:T(256)S(1)} %get-tuple-element.254), channel_id=1, replica_groups=mesh['seq'=64,'head'=4] {'head'}, use_global_device_ids=true, to_apply=%region_8.9 | all-reduce | flops 256 | bytes 2048 | tf_op jit(solution)/shard_map/psum | solution.py:119
  175.2 1.7 multiply_reduce_fusion
  176.9 6.0 %psum.15 = f32[256]{0:T(256)S(1)} all-reduce(f32[256]{0:T(256)S(1)} %multiply_reduce_fusion), channel_id=1, replica_groups=mesh['seq'=64,'head'=4] {'head'}, use_global_device_ids=true, to_apply=%region_10.11 | all-reduce | flops 256 | bytes 2048 | tf_op jit(solution)/shard_map/psum | solution.py:122
  182.9 2.8 multiply_convert_fusion.2
  185.7 1.2 copy.143
  189.3 1.4 fusion.10
  190.7 2.1 copy.135
  192.8 2.5 convolution_bitcast_fusion.4
  195.4 1.3 convolution_bitcast_fusion.5
  196.7 206.6 %all-gather.8.cloned.1.call-done = f32[512,128,128]{2,1,0:T(8,128)} async-done(((f32[8,128,128]{2,1,0:T(8,128)}), f32[512,128,128]{2,1,0:T(8,128)}) %all-gather.8.cloned.1.call-update) | async-done | bytes 33554448 | tf_op jit(solution)/shard_map/all_gather | solution.py:18
  403.4 76.4 %while.17 = (s32[]{:T(128)}, f32[8,128,128]{2,1,0:T(8,128)S(1)}, s32[]{:T(128)}, f32[64,8]{1,0:T(8,128)S(1)}, f32[64,8,128,128]{3,2,1,0:T(8,128)}, /*index=5*/s32[]{:T(128)}, s32[]{:T(128)}, s32[]{:T(128)}, s32[]{:T(128)}) while((s32[]{:T(128)}, f32[8,128,128]{2,1,0:T(8,128)S(1)}, s32[]{:T(128)}, f32[64,8]{1,0:T(8,128)S(1)}, ...), condition=%wide.region_12.13_spmd, body=%wide.region_11.12_spmd.sunk | while | flops 262150 | bytes 1573115 | solution.py:27
  403.4 1.2 bitcast_add_fusion.10
  404.6 1.2 bitcast_add_fusion.10
  405.9 1.2 bitcast_add_fusion.10
  407.1 1.2 bitcast_add_fusion.10
  408.3 1.2 bitcast_add_fusion.10
  409.6 1.2 bitcast_add_fusion.10
  410.8 1.2 bitcast_add_fusion.10
  412.0 1.2 bitcast_add_fusion.10
  413.3 1.2 bitcast_add_fusion.10
  414.5 1.2 bitcast_add_fusion.10
  419.4 1.2 bitcast_add_fusion.10
  420.6 1.2 bitcast_add_fusion.10
  421.9 1.2 bitcast_add_fusion.10
  423.1 1.2 bitcast_add_fusion.10
  424.3 1.2 bitcast_add_fusion.10
  425.6 1.2 bitcast_add_fusion.10
  442.8 1.2 bitcast_add_fusion.10
  444.0 1.2 bitcast_add_fusion.10
  445.3 1.2 bitcast_add_fusion.10
  446.5 1.2 bitcast_add_fusion.10
  447.7 1.2 bitcast_add_fusion.10
  449.0 1.2 bitcast_add_fusion.10
  466.2 1.2 bitcast_add_fusion.10
  467.4 1.2 bitcast_add_fusion.10
  468.7 1.2 bitcast_add_fusion.10
  469.9 1.2 bitcast_add_fusion.10
  471.1 1.2 bitcast_add_fusion.10
  472.4 1.2 bitcast_add_fusion.10
  479.8 1.9 fusion.9
  (155 shorter events, 53.8 us)
Async XLA Ops:
  7.2 7.5 %copy-start = (bf16[256,1024]{1,0:T(8,128)(2,1)S(1)}, bf16[256,1024]{1,0:T(8,128)(2,1)}, u32[]{:S(2)}) copy-start(bf16[256,1024]{1,0:T(8,128)(2,1)} %param.14) | copy-start | bytes 1572868
  7.2 155.0 %all-gather.6.cloned.1.call-start = ((), (), s32[]{:S(2)}) async-start(), calls=%async_computation | async-start | bytes 34078720 | tf_op jit(solution)/shard_map/all_gather | solution.py:18
  11.5 4.4 copy-start.7
  12.7 47.6 %copy-start.5 = (bf16[256,1024]{1,0:T(8,128)(2,1)S(1)}, bf16[256,1024]{1,0:T(8,128)(2,1)}, u32[]{:S(2)}) copy-start(bf16[256,1024]{1,0:T(8,128)(2,1)} %param.13) | copy-start | bytes 1572868
  15.8 387.5 %all-gather.8.cloned.1.call-start = ((), (), s32[]{:S(2)}) async-start(), calls=%async_computation.1 | async-start | bytes 34078720 | tf_op jit(solution)/shard_map/all_gather | solution.py:18
  61.1 1.0 copy-start.1
  163.5 11.7 %copy-start.8 = (f32[1024]{0:T(1024)S(1)}, f32[1024]{0:T(1024)}, u32[]{:S(2)}) copy-start(f32[1024]{0:T(1024)} %param.18) | copy-start | bytes 12292
  188.8 1.9 copy-start.4
  190.7 4.7 copy-start.2
  479.7 3.0 copy-start.3
  479.7 3.0 copy-start.6
Sparse Core Ops, SparseCore 0:
  15.9 146.2 all-gather.5
  188.2 215.1 all-gather.7
where the time goes:
time: 495 us; the launch traced here: 491 us
  waiting for transfers between devices  306 us (62%)
  other arithmetic  82.6 us (17%)
  blocking collectives  58.4 us (12%)
  between operations  15.5 us (3%)
  matrix products  14.2 us (3%)
  local copies, waits for them, and re-layouts  12.1 us (2%)
    all_gather x2, waiting for transfers between devices, prefix(): gathered = jax.tree.map(lambda a: lax.all_gather(a, axis), part)  306 us
    add x63, other arithmetic, link_states(): later[0][:, None, None] * earlier[1] + later[1]  75 us
    all_gather x1, blocking collectives, prefix(): gathered = jax.tree.map(lambda a: lax.all_gather(a, axis), part)  43.9 us
  transfers between devices with their start and end apart: 2, of which 2 were waited for; matrix products, arithmetic and copies ran while one was open for 2% of the time, Pallas kernels for 0%

commit v1 on v0

v1 whole, which is shorter than its diff:
```python
import functools

import jax
import jax.numpy as jnp
from jax import lax
from jax.experimental import pallas as pl
from jax.experimental.pallas import tpu as pltpu
from jax.sharding import PartitionSpec as P

HEAD_DIM = 128
TOK = 256
HALF = 4
EPSILON = 1e-06
HIGHEST = lax.Precision.HIGHEST
F32 = jnp.float32
BF16 = jnp.bfloat16
NEG = -1e30


def dot(a, b, ca, cb, precision=None):
    return lax.dot_general(
        a, b, (((ca,), (cb,)), ((), ())), precision=precision, preferred_element_type=F32
    )


def split(a):
    high = a.astype(BF16)
    return high, (a - high.astype(F32)).astype(BF16)


def call(kernel, outs, n_smem, *args, **kw):
    smem = pl.BlockSpec(memory_space=pltpu.SMEM)
    vmem = pl.BlockSpec(memory_space=pltpu.VMEM)
    return pl.pallas_call(
        kernel,
        out_shape=[jax.ShapeDtypeStruct(s, d) for s, d in outs],
        in_specs=[smem] * n_smem + [vmem] * (len(args) - n_smem),
        out_specs=[vmem] * len(outs),
        compiler_params=pltpu.CompilerParams(vmem_limit_bytes=24 * 1024 * 1024),
        **kw,
    )(*args)


def cols(core, slot):
    return pl.ds(pl.multiple_of(((slot + HALF * core) % 8) * HEAD_DIM, HEAD_DIM), HEAD_DIM)


def here(slot):
    return slice(slot * HEAD_DIM, (slot + 1) * HEAD_DIM)


def first_start(starts):
    return starts[0, 0]


def last_start(starts, place):
    latest = jnp.full_like(place, -1)
    for j in range(4):
        latest = jnp.maximum(latest, jnp.where(starts[0, j] <= place, starts[0, j], -1))
    return latest


def last_of_block(starts):
    latest = jnp.int32(-1)
    for j in range(4):
        latest = jnp.maximum(latest, jnp.where(starts[0, j] < TOK, starts[0, j], -1))
    return latest


def outward_of(starts, summed_col):
    place = lax.broadcasted_iota(jnp.int32, summed_col.shape, 0)
    spread = summed_col[TOK - 1 : TOK, :] - summed_col
    return jnp.exp(jnp.where(place >= last_of_block(starts), spread, NEG))


def inward_of(starts, summed_col):
    place = lax.broadcasted_iota(jnp.int32, summed_col.shape, 0)
    return jnp.exp(jnp.where(place < first_start(starts), summed_col, NEG))


def through_rows(starts, summed_col, slots):
    last = jnp.where(last_of_block(starts) < 0, summed_col[TOK - 1 : TOK, :], NEG)
    factor = jnp.exp(last)
    return [jnp.broadcast_to(factor[:, s : s + 1], (1, HEAD_DIM)) for s in slots]


def weight_of(starts, summed_row, summed_col, slot):
    t = lax.broadcasted_iota(jnp.int32, (TOK, TOK), 0)
    s = lax.broadcasted_iota(jnp.int32, (TOK, TOK), 1)
    keep = jnp.logical_and(s <= t, s >= last_start(starts, t))
    spread = summed_col[:, slot : slot + 1] - summed_row[slot : slot + 1, :]
    return jnp.exp(jnp.where(keep, spread, NEG))


def state_of(left, scale, right):
    scaled = (left.astype(F32) * scale).astype(BF16)
    return dot(scaled, right, 0, 0)


def k_first(core_ref, starts, decay, k, v, send, rows, summed_cols):
    core = core_ref[0]
    d = decay[...]
    d = jnp.where(core == 0, d, jnp.concatenate([d[HALF:], d[:HALF]], axis=0))
    a = lax.broadcasted_iota(jnp.int32, (TOK, TOK), 0)
    b = lax.broadcasted_iota(jnp.int32, (TOK, TOK), 1)
    rows[...] = dot(d, (a <= b).astype(F32), 1, 0, HIGHEST)
    col = dot((b <= a).astype(F32), d, 1, 1, HIGHEST)
    summed_cols[...] = col
    outward = outward_of(starts, col)
    for i in range(HALF):
        at = cols(core, HALF + i)
        send[i * 128 : (i + 1) * 128, :] = state_of(k[:, at], outward[:, HALF + i : HALF + i + 1], v[:, at])
    send[512:520, :] = jnp.concatenate(
        through_rows(starts, col, range(HALF, 8)) + [jnp.zeros((HALF, HEAD_DIM), F32)], axis=0
    )


def k_local(core_ref, starts, rows, summed_cols, q, k, v, mine, within):
    core = core_ref[0]
    row, col = rows[...], summed_cols[...]
    outward = outward_of(starts, col)
    for i in range(HALF):
        at = cols(core, i)
        mine[i * 128 : (i + 1) * 128, :] = state_of(k[:, at], outward[:, i : i + 1], v[:, at])
    mine[512:520, :] = jnp.concatenate(
        through_rows(starts, col, range(HALF)) + [jnp.zeros((HALF, HEAD_DIM), F32)], axis=0
    )
    for slot in range(8):
        at = cols(core, slot)
        scores = dot(q[:, at], k[:, at], 1, 1)
        mixing = (weight_of(starts, row, col, slot) * scores).astype(BF16)
        within[:, here(slot)] = dot(mixing, v[:, at], 1, 0)


def k_pack(core_ref, mine, other, out):
    first = core_ref[0] == 0
    for i in range(HALF):
        at = slice(i * 128, (i + 1) * 128)
        g_mine, g_other = mine[512 + i : 513 + i, :], other[512 + i : 513 + i, :]
        s_mine, s_other = mine[at, :], other[at, :]
        state = jnp.where(first, s_mine * g_other + s_other, s_other * g_mine + s_mine)
        for j in range(8):
            out[8 * i + j, 0:16, :] = state[16 * j : 16 * (j + 1), :]
            out[8 * i + j, 16:24, :] = jnp.broadcast_to(g_mine * g_other, (8, HEAD_DIM))


def k_scan(pieces, out):
    state = jnp.zeros((16, HEAD_DIM), F32)
    for i in range(32):
        out[i] = state
        state = state * pieces[i, 16:17, :] + pieces[i, 0:16, :]


def k_scan_back(pieces, factors, out):
    state = jnp.zeros((16, HEAD_DIM), F32)
    for i in reversed(range(32)):
        out[i] = state
        state = state * factors[i, 16:17, :] + pieces[i]


def k_enter(core_ref, entering, mine, other, e_mine, e_send):
    first = core_ref[0] == 0
    for i in range(HALF):
        at = slice(i * 128, (i + 1) * 128)
        g0 = jnp.where(first, mine[512 + i : 513 + i, :], other[512 + i : 513 + i, :])
        s0 = jnp.where(first, mine[at, :], other[at, :])
        e0 = entering[at, :]
        e1 = e0 * g0 + s0
        e_mine[at, :] = jnp.where(first, e0, e1)
        e_send[at, :] = jnp.where(first, e1, e0)


def k_attend(core_ref, starts, summed_cols, q, within, e_mine, out):
    core = core_ref[0]
    inward = inward_of(starts, summed_cols[...])
    for i in range(HALF):
        high, low = split(e_mine[i * 128 : (i + 1) * 128, :])
        query = q[:, cols(core, i)]
        carried = dot(query, high, 1, 0) + dot(query, low, 1, 0)
        out[:, here(i)] = within[:, here(i)] + carried * inward[:, i : i + 1]


def k_sums(core_ref, starts, summed_cols, q, within, e_other, att_mine, gate, gain, up, att_other, sums):
    core = core_ref[0]
    inward = inward_of(starts, summed_cols[...])
    squares = jnp.zeros((TOK, HEAD_DIM), F32)
    products = jnp.zeros((TOK, HEAD_DIM), F32)
    for slot in range(8):
        at = cols(core, slot)
        if slot < HALF:
            att = att_mine[:, here(slot)]
        else:
            i = slot - HALF
            high, low = split(e_other[i * 128 : (i + 1) * 128, :])
            query = q[:, at]
            carried = dot(query, high, 1, 0) + dot(query, low, 1, 0)
            att = within[:, here(slot)] + carried * inward[:, slot : slot + 1]
            att_other[:, here(i)] = att
        dnormed = up[:, at].astype(F32) * gain[:, at] * jax.nn.sigmoid(gate[:, at].astype(F32))
        squares += att * att
        products += dnormed * att
    ones = jnp.ones((8, HEAD_DIM), F32)
    line = lax.broadcasted_iota(jnp.int32, (8, TOK), 0)
    both = jnp.where(line < 4, dot(ones, squares, 1, 1, HIGHEST), dot(ones, products, 1, 1, HIGHEST))
    for j in range(4):
        sums[j] = both


def k_grad(core_ref, starts, summed_cols, sums, att_mine, att_other, gate, gain, up, q, grad, send, grad_gate, *, features):
    core = core_ref[0]
    inward = inward_of(starts, summed_cols[...])
    total = sums[0] + sums[1] + sums[2] + sums[3]
    line = lax.broadcasted_iota(jnp.int32, (8, HEAD_DIM), 0)
    squares = dot(total, (line == 0).astype(F32), 0, 0, HIGHEST)
    products = dot(total, (line == 4).astype(F32), 0, 0, HIGHEST)
    inverse = 1.0 / jnp.sqrt(squares / features + EPSILON)
    projection = products * inverse / features
    for slot in reversed(range(8)):
        at = cols(core, slot)
        att = att_mine[:, here(slot)] if slot < HALF else att_other[:, here(slot - HALF)]
        opening = jax.nn.sigmoid(gate[:, at].astype(F32))
        dnormed = up[:, at].astype(F32) * gain[:, at] * opening
        normed = att * inverse
        grad_gate[:, at] = (dnormed * normed * (1.0 - opening)).astype(BF16)
        value = ((dnormed - normed * projection) * inverse).astype(BF16)
        grad[:, here(slot)] = value
        if slot >= HALF:
            i = slot - HALF
            send[i * 128 : (i + 1) * 128, :] = state_of(q[:, at], inward[:, slot : slot + 1], value)


def k_back(core_ref, starts, rows, summed_cols, q, k, v, grad, e_mine, e_other, mine, gq, gk, gv):
    core = core_ref[0]
    row, col = rows[...], summed_cols[...]
    inward = inward_of(starts, col)
    for slot in range(8):
        at = cols(core, slot)
        query, key, value, upstream = q[:, at], k[:, at], v[:, at], grad[:, here(slot)]
        i = slot % HALF
        if slot < HALF:
            mine[i * 128 : (i + 1) * 128, :] = state_of(query, inward[:, slot : slot + 1], upstream)
        weight = weight_of(starts, row, col, slot)
        mixing = (weight * dot(query, key, 1, 1)).astype(BF16)
        grad_mixing = (weight * dot(upstream, value, 1, 1)).astype(BF16)
        state = (e_mine if slot < HALF else e_other)[i * 128 : (i + 1) * 128, :]
        high, low = split(state)
        carried = dot(upstream, high, 1, 1) + dot(upstream, low, 1, 1)
        gq[:, at] = (dot(grad_mixing, key, 1, 0) + carried * inward[:, slot : slot + 1]).astype(BF16)
        gk[:, here(slot)] = dot(grad_mixing, query, 0, 0)
        gv[:, here(slot)] = dot(mixing, upstream, 0, 0)


def k_pack_back(core_ref, mine, other, s_mine, s_other, out):
    first = core_ref[0] == 0
    for i in range(HALF):
        at = slice(i * 128, (i + 1) * 128)
        g0 = jnp.where(first, s_mine[512 + i : 513 + i, :], s_other[512 + i : 513 + i, :])
        b_mine, b_other = mine[at, :], other[at, :]
        state = jnp.where(first, b_mine + g0 * b_other, b_other + g0 * b_mine)
        for j in range(8):
            out[8 * i + j] = state[16 * j : 16 * (j + 1), :]


def k_leave(core_ref, leaving, mine, other, s_mine, s_other, l_mine, l_send):
    first = core_ref[0] == 0
    for i in range(HALF):
        at = slice(i * 128, (i + 1) * 128)
        g1 = jnp.where(first, s_other[512 + i : 513 + i, :], s_mine[512 + i : 513 + i, :])
        b1 = jnp.where(first, other[at, :], mine[at, :])
        l1 = leaving[at, :]
        l0 = l1 * g1 + b1
        l_mine[at, :] = jnp.where(first, l0, l1)
        l_send[at, :] = jnp.where(first, l1, l0)


def finish(core, slot, state, outward, k, v, gk, gv):
    at = cols(core, slot)
    high, low = split(state)
    value, key = v[:, at], k[:, at]
    scale = outward[:, slot : slot + 1]
    to_key = dot(value, high, 1, 1) + dot(value, low, 1, 1)
    to_value = dot(key, high, 1, 0) + dot(key, low, 1, 0)
    return (
        (gk[:, here(slot)] + to_key * scale).astype(BF16),
        (gv[:, here(slot)] + to_value * scale).astype(BF16),
    )


def k_end_mine(core_ref, starts, summed_cols, k, v, gk, gv, l_mine, out_k, out_v):
    core = core_ref[0]
    outward = outward_of(starts, summed_cols[...])
    for i in range(HALF):
        state = l_mine[i * 128 : (i + 1) * 128, :]
        out_k[:, here(i)], out_v[:, here(i)] = finish(core, i, state, outward, k, v, gk, gv)


def k_end(core_ref, starts, summed_cols, k, v, gk, gv, l_other, k_mine, v_mine, out_k, out_v):
    core = core_ref[0]
    outward = outward_of(starts, summed_cols[...])
    for i in range(HALF):
        at = cols(core, i)
        out_k[:, at] = k_mine[:, here(i)]
        out_v[:, at] = v_mine[:, here(i)]
    for i in range(HALF):
        at = cols(core, HALF + i)
        state = l_other[i * 128 : (i + 1) * 128, :]
        out_k[:, at], out_v[:, at] = finish(core, HALF + i, state, outward, k, v, gk, gv)


def local(q, k, v, decay, starts, gate, gain, up):
    places = lax.axis_size("seq")
    swap = [(i, i ^ 1) for i in range(places)]
    groups = [list(range(c, places, 2)) for c in range(2)]
    core = (lax.axis_index("seq") % 2).astype(jnp.int32).reshape(1)
    features = q.shape[1] * lax.axis_size("head")
    gain = gain.reshape(1, -1)
    wide, half = (TOK, 1024), (TOK, 512)
    state, state_g = (512, HEAD_DIM), (520, HEAD_DIM)

    def trade(a):
        return lax.all_to_all(a, "seq", 0, 0, axis_index_groups=groups)

    send, rows, summed = call(
        k_first, [(state_g, F32), ((8, TOK), F32), ((TOK, 8), F32)], 2, core, starts, decay, k, v
    )
    s_other = lax.ppermute(send, "seq", swap)
    s_mine, within = call(k_local, [(state_g, F32), (wide, F32)], 2, core, starts, rows, summed, q, k, v)
    (pieces,) = call(k_pack, [((32, 24, HEAD_DIM), F32)], 1, core, s_mine, s_other)
    pieces = trade(pieces)
    (entering,) = call(k_scan, [((32, 16, HEAD_DIM), F32)], 0, pieces)
    entering = trade(entering).reshape(state)
    e_mine, e_send = call(k_enter, [(state, F32)] * 2, 1, core, entering, s_mine, s_other)
    e_other = lax.ppermute(e_send, "seq", swap)
    (att_mine,) = call(k_attend, [(half, F32)], 2, core, starts, summed, q, within, e_mine)
    att_other, sums = call(
        k_sums,
        [(half, F32), ((4, 8, TOK), F32)],
        2, core, starts, summed, q, within, e_other, att_mine, gate, gain, up,
    )
    sums = lax.all_to_all(sums, "head", 0, 0)
    grad, b_send, grad_gate = call(
        functools.partial(k_grad, features=float(features)),
        [(wide, BF16), (state, F32), (wide, BF16)],
        2, core, starts, summed, sums, att_mine, att_other, gate, gain, up, q,
    )
    b_other = lax.ppermute(b_send, "seq", swap)
    b_mine, gq, gk, gv = call(
        k_back,
        [(state, F32), (wide, BF16), (wide, F32), (wide, F32)],
        2, core, starts, rows, summed, q, k, v, grad, e_mine, e_other,
    )
    (back,) = call(k_pack_back, [((32, 16, HEAD_DIM), F32)], 1, core, b_mine, b_other, s_mine, s_other)
    back = trade(back)
    (leaving,) = call(k_scan_back, [((32, 16, HEAD_DIM), F32)], 0, back, pieces)
    leaving = trade(leaving).reshape(state)
    l_mine, l_send = call(k_leave, [(state, F32)] * 2, 1, core, leaving, b_mine, b_other, s_mine, s_other)
    l_other = lax.ppermute(l_send, "seq", swap)
    k_mine, v_mine = call(k_end_mine, [(half, BF16)] * 2, 2, core, starts, summed, k, v, gk, gv, l_mine)
    grad_key, grad_value = call(
        k_end, [(wide, BF16)] * 2, 2, core, starts, summed, k, v, gk, gv, l_other, k_mine, v_mine
    )
    return gq, grad_key, grad_value, grad_gate


def solution(mesh):
    token = P("seq", "head")
    return jax.shard_map(
        local,
        mesh=mesh,
        in_specs=(token, token, token, P("head", "seq"), P("seq", None), token, P("head"), token),
        out_specs=(token,) * 4,
        check_vma=False,
    )
```

time: 495 us -> 111 us (0.22)
  waiting for transfers between devices: 306 us -> 0.44 us
  other arithmetic: 82.6 us -> 0 us
  blocking collectives: 58.4 us -> 76.5 us
  Pallas kernels: 0 us -> 16.6 us
  between operations: 15.5 us -> 0.73 us
  matrix products: 14.2 us -> 0 us
  starting transfers between devices: 0.08 us -> 12.5 us
  local copies, waits for them, and re-layouts: 12.1 us -> 3.86 us
    all_gather x2 -> x0, waiting for transfers between devices: 306 us -> none  [prefix(): gathered = jax.tree.map(lambda a: lax.all_gather(a, axis), part)]
    all_to_all x0 -> x5, blocking collectives: none -> 76.5 us  [the longest x4 68.2 us: trade(): return lax.all_to_all(a, 'seq', 0, 0, axis_index_groups=groups)]
    add x63 -> x0, other arithmetic: 75 us -> none  [link_states(): later[0][:, None, None] * earlier[1] + later[1]]
    all_gather x1 -> x0, blocking collectives: 43.9 us -> none  [prefix(): gathered = jax.tree.map(lambda a: lax.all_gather(a, axis), part)]
    pallas_call x0 -> x14, Pallas kernels: none -> 16.6 us  [call(): pl.pallas_call(kernel, out_shape=[jax.ShapeDtypeStruct(s, d) for s, d in...]
    psum x2 -> x0, blocking collectives: 14.5 us -> none  [the longest x1 8.46 us: local(): totals = lax.psum(squares, 'head')]
    dot_general x12 -> x0, matrix products: 14.2 us -> none  [the longest x1 2.52 us: local(): jnp.einsum('nhts,nthd->nshd', grad_mixing, query_blocks, preferred_elemen...]
    ppermute x0 -> x4, starting transfers between devices: none -> 12.5 us  [the longest x1 3.74 us: local(): e_other = lax.ppermute(e_send, 'seq', swap)]
  transfers between devices with their start and end apart: 2 -> 4, of which waited for: 2 -> 2; matrix products, arithmetic and copies ran while one was open for 2% -> 0% of each run, Pallas kernels for 0% -> 8%
where the time goes in v1:
time: 111 us
  blocking collectives  76.5 us (69%)
  Pallas kernels  16.6 us (15%)
  starting transfers between devices  12.5 us (11%)
  local copies, waits for them, and re-layouts  3.86 us (3%)
    all_to_all x4, blocking collectives, trade(): return lax.all_to_all(a, 'seq', 0, 0, axis_index_groups=groups)  68.2 us
    pallas_call x14, Pallas kernels, call(): pl.pallas_call(kernel, out_shape=[jax.ShapeDtypeStruct(s, d) for s, d in...  16.6 us
    all_to_all x1, blocking collectives, local(): sums = lax.all_to_all(sums, 'head', 0, 0)  8.29 us
    unnamed x22, local copies, waits for them, and re-layouts  3.86 us
    ppermute x1, starting transfers between devices, local(): e_other = lax.ppermute(e_send, 'seq', swap)  3.74 us
    ppermute x1, starting transfers between devices, local(): l_other = lax.ppermute(l_send, 'seq', swap)  3.7 us
    ppermute x1, starting transfers between devices, local(): s_other = lax.ppermute(send, 'seq', swap)  3.33 us
  transfers between devices with their start and end apart: 4, of which 2 were waited for; matrix products, arithmetic and copies ran while one was open for 0% of the time, Pallas kernels for 8%

profile of v1, /device:TPU:1, one launch (start us, length us, event | category | flops | bytes accessed | tf_op | source)
XLA Modules:
  0.0 110.7 jit_solution(2573422041709920533)
XLA Ops:
  0.6 0.0 copy-start.10
  0.7 0.0 copy-start.8
  0.7 0.7 copy-done.10
  1.3 0.0 copy-done.8
  1.3 0.0 copy-start.1
  1.3 1.0 copy-done.1
  2.4 0.0 copy-start.3
  2.4 1.0 copy-done.3
  3.4 0.0 copy-start
  3.4 0.0 copy-start.2
  3.4 1.5 %shard_map.111 = (f32[520,128]{1,0:T(8,128)S(1)}, f32[8,256]{1,0:T(8,128)S(1)}, f32[256,8]{1,0:T(8,128)S(1)}) custom-call(s32[1]{0:T(128)} %bitcast.core_ref, s32[1,4]{1,0:T(1,128)S(1)} %copy-done.8, f32[8,256]{1,0:T(8,128)S(1)} %copy-done.10, bf16[256,1024]{1,0:T(8,128)(2,1)S(1)} %copy-done.1, bf16[256,1024]{1,0:T(8,128)(2,1)S(1)} %copy-done.3), custom_call_target="tpu_custom_call" | custom-call | tf_op jit(solution)/shard_map/pallas_call | solution.py:34
  4.9 3.3 %collective-permute-start = (f32[520,128]{1,0:T(8,128)S(1)}, f32[520,128]{1,0:T(8,128)S(1)}, u32[]{:S(2)}, u32[]{:S(2)}) collective-permute-start(f32[520,128]{1,0:T(8,128)S(1)} %get-tuple-element.30), channel_id=1, source_target_pairs={{0,4},{4,0},{8,12},{12,8},{16,20},{20,16},{24,28},{28,24},{32,36},... | collective-permute-start | bytes 798728 | tf_op jit(solution)/shard_map/ppermute | solution.py:326
  8.3 0.0 copy-done
  8.3 0.0 copy-done.2
  8.3 0.0 copy-start.4
  8.3 1.0 copy-done.4
  9.3 2.4 %shard_map.112 = (f32[520,128]{1,0:T(8,128)S(1)}, f32[256,1024]{1,0:T(8,128)S(1)}) custom-call(s32[1]{0:T(128)} %bitcast.core_ref, s32[1,4]{1,0:T(1,128)S(1)} %copy-done.8, f32[8,256]{1,0:T(8,128)S(1)} %get-tuple-element.26.rows, f32[256,8]{1,0:T(8,128)S(1)} %get-tuple-element.27.summed_cols, bf16[256,1024]{1,0:T(8,128)(2,1)S(1)} %copy-done, ...), custom_call_target="tpu_custom_call" | custom-call | tf_op jit(solution)/shard_map/pallas_call | solution.py:34
  11.8 0.0 collective-permute-done.other.s_other
  11.8 0.1 shard_map.113
  11.8 21.3 %all_to_all.25.pieces.factors = f32[32,24,128]{2,1,0:T(8,128)S(1)} all-to-all(f32[32,24,128]{2,1,0:T(8,128)S(1)} %shard_map.113), channel_id=1, replica_groups={{0,8,16,24,32,40,48,56,64,72,80,88,96,104,112,120,128,136,144,152,160,1..., dimensions={0} | all-to-all | bytes 786432 | tf_op jit(solution)/shard_map/all_to_all | solution.py:321
  33.1 0.1 shard_map.114
  33.2 16.8 %all_to_all.26 = f32[32,16,128]{2,1,0:T(8,128)S(1)} all-to-all(f32[32,16,128]{2,1,0:T(8,128)S(1)} %shard_map.114), channel_id=1, replica_groups={{0,8,16,24,32,40,48,56,64,72,80,88,96,104,112,120,128,136,144,152,160,1..., dimensions={0} | all-to-all | bytes 524288 | tf_op jit(solution)/shard_map/all_to_all | solution.py:321
  50.0 0.1 shard_map.115
  50.1 3.7 %collective-permute-start.1 = (f32[512,128]{1,0:T(8,128)S(1)}, f32[512,128]{1,0:T(8,128)S(1)}, u32[]{:S(2)}, u32[]{:S(2)}) collective-permute-start(f32[512,128]{1,0:T(8,128)S(1)} %get-tuple-element.31), channel_id=1, source_target_pairs={{0,4},{4,0},{8,12},{12,8},{16,20},{20,16},{24,28},{28,24},{32,36},... | collective-permute-start | bytes 786440 | tf_op jit(solution)/shard_map/ppermute | solution.py:333
  53.8 0.0 copy-start.6
  53.8 0.0 copy-start.7
  53.8 0.0 copy-start.9
  53.8 0.8 shard_map.116.att_mine
  54.7 0.3 collective-permute-done.1.e_other
  55.0 0.0 copy-done.6
  55.0 0.0 copy-done.7
  55.0 0.0 copy-done.9
  55.0 1.4 %shard_map.117 = (f32[256,512]{1,0:T(8,128)S(1)}, f32[4,8,256]{2,1,0:T(8,128)S(1)}) custom-call(s32[1]{0:T(128)} %bitcast.core_ref, s32[1,4]{1,0:T(1,128)S(1)} %copy-done.8, f32[256,8]{1,0:T(8,128)S(1)} %get-tuple-element.27.summed_cols, bf16[256,1024]{1,0:T(8,128)(2,1)S(1)} %copy-done, f32[256,1024]{1,0:T(8,128)S(1)} %get-tuple-element.28.within, ...), custom_call_target="tpu_custom_call" | custom-call | tf_op jit(solution)/shard_map/pallas_call | solution.py:34
  56.5 8.3 %all_to_all.27.sums = f32[4,8,256]{2,1,0:T(8,128)S(1)} all-to-all(f32[4,8,256]{2,1,0:T(8,128)S(1)} %get-tuple-element.33), channel_id=1, replica_groups=mesh['seq'=64,'head'=4] {'head'}, dimensions={0} | all-to-all | bytes 65536 | tf_op jit(solution)/shard_map/all_to_all | solution.py:340
  64.8 2.5 %shard_map.118 = (bf16[256,1024]{1,0:T(8,128)(2,1)S(1)}, f32[512,128]{1,0:T(8,128)S(1)}, bf16[256,1024]{1,0:T(8,128)(2,1)}) custom-call(s32[1]{0:T(128)} %bitcast.core_ref, s32[1,4]{1,0:T(1,128)S(1)} %copy-done.8, f32[256,8]{1,0:T(8,128)S(1)} %get-tuple-element.27.summed_cols, f32[4,8,256]{2,1,0:T(8,128)S(1)} %all_to_all.27.sums, ...), custom_call_target="tpu_custom_call" | custom-call | tf_op jit(solution)/shard_map/pallas_call | solution.py:34
  67.3 1.8 %collective-permute-start.2 = (f32[512,128]{1,0:T(8,128)S(1)}, f32[512,128]{1,0:T(8,128)S(1)}, u32[]{:S(2)}, u32[]{:S(2)}) collective-permute-start(f32[512,128]{1,0:T(8,128)S(1)} %get-tuple-element.40), channel_id=1, source_target_pairs={{0,4},{4,0},{8,12},{12,8},{16,20},{20,16},{24,28},{28,24},{32,36},... | collective-permute-start | bytes 786440 | tf_op jit(solution)/shard_map/ppermute | solution.py:346
  69.0 0.0 copy-done.5
  69.0 4.5 %shard_map.119 = (f32[512,128]{1,0:T(8,128)S(1)}, bf16[256,1024]{1,0:T(8,128)(2,1)}, f32[256,1024]{1,0:T(8,128)S(1)}, f32[256,1024]{1,0:T(8,128)S(1)}) custom-call(s32[1]{0:T(128)} %bitcast.core_ref, s32[1,4]{1,0:T(1,128)S(1)} %copy-done.8, f32[8,256]{1,0:T(8,128)S(1)} %get-tuple-element.26.rows, f32[256,8]{1,0:T(8,128)S(1)} %get-tuple-element.27.summed_cols, ...), custom_call_target="tpu_custom_call" | custom-call | tf_op jit(solution)/shard_map/pallas_call | solution.py:34
  73.5 0.0 collective-permute-done.2.other
  73.5 0.1 shard_map.120
  73.6 14.4 %all_to_all.28.pieces = f32[32,16,128]{2,1,0:T(8,128)S(1)} all-to-all(f32[32,16,128]{2,1,0:T(8,128)S(1)} %shard_map.120), channel_id=1, replica_groups={{0,8,16,24,32,40,48,56,64,72,80,88,96,104,112,120,128,136,144,152,160,1..., dimensions={0} | all-to-all | bytes 524288 | tf_op jit(solution)/shard_map/all_to_all | solution.py:321
  87.9 0.1 shard_map.121
  88.0 15.7 %all_to_all.29 = f32[32,16,128]{2,1,0:T(8,128)S(1)} all-to-all(f32[32,16,128]{2,1,0:T(8,128)S(1)} %shard_map.121), channel_id=1, replica_groups={{0,8,16,24,32,40,48,56,64,72,80,88,96,104,112,120,128,136,144,152,160,1..., dimensions={0} | all-to-all | bytes 524288 | tf_op jit(solution)/shard_map/all_to_all | solution.py:321
  103.7 0.1 shard_map.122
  103.8 3.7 %collective-permute-start.3 = (f32[512,128]{1,0:T(8,128)S(1)}, f32[512,128]{1,0:T(8,128)S(1)}, u32[]{:S(2)}, u32[]{:S(2)}) collective-permute-start(f32[512,128]{1,0:T(8,128)S(1)} %get-tuple-element.41), channel_id=1, source_target_pairs={{0,4},{4,0},{8,12},{12,8},{16,20},{20,16},{24,28},{28,24},{32,36},... | collective-permute-start | bytes 786440 | tf_op jit(solution)/shard_map/ppermute | solution.py:357
  107.5 1.0 shard_map.123
  108.5 0.1 collective-permute-done.3.l_other
  108.6 2.1 %shard_map.124 = (bf16[256,1024]{1,0:T(8,128)(2,1)}, bf16[256,1024]{1,0:T(8,128)(2,1)}) custom-call(s32[1]{0:T(128)} %bitcast.core_ref, s32[1,4]{1,0:T(1,128)S(1)} %copy-done.8, f32[256,8]{1,0:T(8,128)S(1)} %get-tuple-element.27.summed_cols, bf16[256,1024]{1,0:T(8,128)(2,1)S(1)} %copy-done.2, bf16[256,1024]{1,0:T(8,128)(2,1)S(1)} %copy-done.5, ...), custom_call_target="tpu_custom_call" | custom-call | tf_op jit(solution)/shard_map/pallas_call | solution.py:34
  (1 shorter events, 0.0 us)
Async XLA Ops:
  0.6 0.7 copy-start.10
  0.7 0.7 copy-start.8
  1.3 1.0 copy-start.1
  2.4 1.0 copy-start.3
  3.4 4.9 %copy-start = (bf16[256,1024]{1,0:T(8,128)(2,1)S(1)}, bf16[256,1024]{1,0:T(8,128)(2,1)}, u32[]{:S(2)}) copy-start(bf16[256,1024]{1,0:T(8,128)(2,1)} %q.9) | copy-start | bytes 1572868
  3.4 4.9 %copy-start.2 = (bf16[256,1024]{1,0:T(8,128)(2,1)S(1)}, bf16[256,1024]{1,0:T(8,128)(2,1)}, u32[]{:S(2)}) copy-start(bf16[256,1024]{1,0:T(8,128)(2,1)} %k.9) | copy-start | bytes 1572868
  4.9 6.8 %collective-permute-start = (f32[520,128]{1,0:T(8,128)S(1)}, f32[520,128]{1,0:T(8,128)S(1)}, u32[]{:S(2)}, u32[]{:S(2)}) collective-permute-start(f32[520,128]{1,0:T(8,128)S(1)} %get-tuple-element.30), channel_id=1, source_target_pairs={{0,4},{4,0},{8,12},{12,8},{16,20},{20,16},{24,28},{28,24},{32,36},... | collective-permute-start | bytes 798728 | tf_op jit(solution)/shard_map/ppermute | solution.py:326
  8.3 1.0 copy-start.4
  50.1 4.9 %collective-permute-start.1 = (f32[512,128]{1,0:T(8,128)S(1)}, f32[512,128]{1,0:T(8,128)S(1)}, u32[]{:S(2)}, u32[]{:S(2)}) collective-permute-start(f32[512,128]{1,0:T(8,128)S(1)} %get-tuple-element.31), channel_id=1, source_target_pairs={{0,4},{4,0},{8,12},{12,8},{16,20},{20,16},{24,28},{28,24},{32,36},... | collective-permute-start | bytes 786440 | tf_op jit(solution)/shard_map/ppermute | solution.py:333
  53.8 1.2 %copy-start.6 = (bf16[256,1024]{1,0:T(8,128)(2,1)S(1)}, bf16[256,1024]{1,0:T(8,128)(2,1)}, u32[]{:S(2)}) copy-start(bf16[256,1024]{1,0:T(8,128)(2,1)} %gate.3) | copy-start | bytes 1572868
  53.8 1.2 %copy-start.7 = (bf16[256,1024]{1,0:T(8,128)(2,1)S(1)}, bf16[256,1024]{1,0:T(8,128)(2,1)}, u32[]{:S(2)}) copy-start(bf16[256,1024]{1,0:T(8,128)(2,1)} %up.3) | copy-start | bytes 1572868
  53.8 1.2 %copy-start.9 = (f32[1024]{0:T(1024)S(1)}, f32[1024]{0:T(1024)}, u32[]{:S(2)}) copy-start(f32[1024]{0:T(1024)} %param.14) | copy-start | bytes 12292
  64.8 4.3 %copy-start.5 = (bf16[256,1024]{1,0:T(8,128)(2,1)S(1)}, bf16[256,1024]{1,0:T(8,128)(2,1)}, u32[]{:S(2)}) copy-start(bf16[256,1024]{1,0:T(8,128)(2,1)} %v.9) | copy-start | bytes 1572868
  67.3 6.2 %collective-permute-start.2 = (f32[512,128]{1,0:T(8,128)S(1)}, f32[512,128]{1,0:T(8,128)S(1)}, u32[]{:S(2)}, u32[]{:S(2)}) collective-permute-start(f32[512,128]{1,0:T(8,128)S(1)} %get-tuple-element.40), channel_id=1, source_target_pairs={{0,4},{4,0},{8,12},{12,8},{16,20},{20,16},{24,28},{28,24},{32,36},... | collective-permute-start | bytes 786440 | tf_op jit(solution)/shard_map/ppermute | solution.py:346
  103.8 4.9 %collective-permute-start.3 = (f32[512,128]{1,0:T(8,128)S(1)}, f32[512,128]{1,0:T(8,128)S(1)}, u32[]{:S(2)}, u32[]{:S(2)}) collective-permute-start(f32[512,128]{1,0:T(8,128)S(1)} %get-tuple-element.41), channel_id=1, source_target_pairs={{0,4},{4,0},{8,12},{12,8},{16,20},{20,16},{24,28},{28,24},{32,36},... | collective-permute-start | bytes 786440 | tf_op jit(solution)/shard_map/ppermute | solution.py:357

commit v2 on v1

v2 whole, which is shorter than its diff:
```python
import functools

import jax
import jax.numpy as jnp
from jax import lax
from jax.experimental import pallas as pl
from jax.experimental.pallas import tpu as pltpu
from jax.sharding import PartitionSpec as P

HEAD_DIM = 128
TOK = 256
HALF = 4
EPSILON = 1e-06
F32 = jnp.float32
BF16 = jnp.bfloat16
NEG = -1e30


def dot(a, b, ca, cb):
    return lax.dot_general(a, b, (((ca,), (cb,)), ((), ())), preferred_element_type=F32)


def parts(a, count):
    out = []
    for _ in range(count):
        out.append(a.astype(BF16))
        a = a - out[-1].astype(F32)
    return out


def wide_dot(a, state, axis):
    return dot(jnp.concatenate([a, a], axis=1), jnp.concatenate(parts(state, 2), axis=axis), 1, axis)


def call(kernel, outs, n_smem, *args, hbm=(), hbm_out=(), scratch=(), vmem_mib=24, **kw):
    smem = pl.BlockSpec(memory_space=pltpu.SMEM)
    vmem = pl.BlockSpec(memory_space=pltpu.VMEM)
    far = pl.BlockSpec(memory_space=pltpu.HBM)
    return pl.pallas_call(
        kernel,
        out_shape=[jax.ShapeDtypeStruct(s, d) for s, d in outs],
        in_specs=[smem] * n_smem + [far if n in hbm else vmem for n in range(n_smem, len(args))],
        out_specs=[far if n in hbm_out else vmem for n in range(len(outs))],
        scratch_shapes=list(scratch),
        compiler_params=pltpu.CompilerParams(vmem_limit_bytes=int(vmem_mib * 1024 * 1024)),
        **kw,
    )(*args)


def cols(core, slot):
    return pl.ds(pl.multiple_of(((slot + HALF * core) % 8) * HEAD_DIM, HEAD_DIM), HEAD_DIM)


def half_cols(half):
    width = HALF * HEAD_DIM
    return pl.ds(pl.multiple_of(half * width, width), width)


def here(slot):
    return slice(slot * HEAD_DIM, (slot + 1) * HEAD_DIM)


def spread(lines, count):
    n = lines.shape[0]
    shape = (count * n, n * HEAD_DIM)
    line = lax.broadcasted_iota(jnp.int32, shape, 0) % n
    head = lax.broadcasted_iota(jnp.int32, shape, 1) // HEAD_DIM
    pick = (line == head).astype(F32).astype(BF16)
    return dot(jnp.concatenate(parts(lines, count), axis=0), pick, 0, 0)


def latest_of(rows):
    return rows[8:9, :]


def outward_of(rows, slots):
    row, latest = rows[slots, :], latest_of(rows)
    place = lax.broadcasted_iota(jnp.int32, row.shape, 1).astype(F32)
    kept = place >= latest[:, TOK - 1 : TOK]
    return jnp.exp(jnp.where(kept, row[:, TOK - 1 : TOK] - row, NEG))


def inward_of(rows):
    return jnp.exp(jnp.where(latest_of(rows) < 0, rows[0:8, :], NEG))


def through_of(rows):
    last = jnp.where(latest_of(rows)[:, TOK - 1 : TOK] < 0, rows[0:8, TOK - 1 : TOK], NEG)
    return jnp.broadcast_to(jnp.exp(last), (8, HEAD_DIM))


def state_of(left, scale, right):
    return dot((left.astype(F32) * scale).astype(BF16), right, 0, 0)


def fetch(pairs, sems):
    copies = [pltpu.make_async_copy(src, dst, sems.at[n]) for n, (src, dst) in enumerate(pairs)]
    for copy in copies:
        copy.start()
    return copies


def k_first(core_ref, aux, k, v, send, rows, kbuf, vbuf, sems):
    core = core_ref[0]
    there = half_cols(1 - core)
    copies = fetch([(k.at[:, there], kbuf), (v.at[:, there], vbuf)], sems)
    a = lax.broadcasted_iota(jnp.int32, (TOK, TOK), 0)
    b = lax.broadcasted_iota(jnp.int32, (TOK, TOK), 1)
    d = aux[0:8, :]
    d = jnp.where(core == 0, d, jnp.concatenate([d[HALF:], d[:HALF]], axis=0))
    sums = dot(jnp.concatenate(parts(d, 3), axis=0), (a <= b).astype(BF16), 1, 0)
    rows[0:8, :] = sums[0:8] + sums[8:16] + sums[16:24]
    place = lax.broadcasted_iota(jnp.int32, (1, TOK), 1).astype(F32)
    latest = jnp.full((1, TOK), -1.0, F32)
    for j in range(4):
        begin = aux[8:9, j : j + 1]
        latest = jnp.maximum(latest, jnp.where(begin <= place, begin, -1.0))
    rows[8:16, :] = jnp.broadcast_to(latest, (8, TOK))
    outward = spread(outward_of(rows, slice(HALF, 8)), 2)
    through = through_of(rows)
    send[512:520, :] = jnp.concatenate([through[HALF:8], through[0:HALF]], axis=0)
    for copy in copies:
        copy.wait()
    for i in range(HALF):
        send[i * 128 : (i + 1) * 128, :] = state_of(kbuf[:, here(i)], outward[:, here(i)], vbuf[:, here(i)])


def mixed(weight, query, key, value):
    return dot((weight * dot(query, key, 1, 1)).astype(BF16), value, 1, 0)


def biases(rows):
    latest = spread(latest_of(rows), 1)
    t = lax.broadcasted_iota(jnp.int32, (TOK, HEAD_DIM), 0)
    s = lax.broadcasted_iota(jnp.int32, (TOK, HEAD_DIM), 1)
    out = []
    for part in range(2):
        place = s + part * HEAD_DIM
        out.append(jnp.where(jnp.logical_and(place <= t, place.astype(F32) >= latest), 0.0, NEG))
    return out


def weight_of(rows, column, bias, slot):
    line = rows[slot : slot + 1, :]
    return jnp.concatenate(
        [jnp.exp(column - line[:, here(part)] + bias[part]) for part in range(2)], axis=1
    )


def k_local(core_ref, rows, q, k, v, mine, within, qbuf, kbuf, vbuf, sems):
    core = core_ref[0]
    there = half_cols(core)
    copies = fetch([(k.at[:, there], kbuf), (v.at[:, there], vbuf), (q.at[:, there], qbuf)], sems)
    columns = spread(rows[0:HALF, :], 3)
    bias = biases(rows)
    outward = spread(outward_of(rows, slice(0, HALF)), 2)
    mine[512:520, :] = through_of(rows)
    copies[0].wait()
    copies[1].wait()
    for i in range(HALF):
        mine[i * 128 : (i + 1) * 128, :] = state_of(kbuf[:, here(i)], outward[:, here(i)], vbuf[:, here(i)])
    copies[2].wait()
    for i in range(HALF):
        weight = weight_of(rows, columns[:, here(i)], bias, i)
        within[:, here(i)] = mixed(weight, qbuf[:, here(i)], kbuf[:, here(i)], vbuf[:, here(i)])


def k_pack(core_ref, mine, other, out):
    first = core_ref[0] == 0
    for i in range(HALF):
        at = slice(i * 128, (i + 1) * 128)
        g_mine, g_other = mine[512 + i : 513 + i, :], other[512 + i : 513 + i, :]
        s_mine, s_other = mine[at, :], other[at, :]
        state = jnp.where(first, s_mine * g_other + s_other, s_other * g_mine + s_mine)
        for j in range(8):
            base = 17 * (8 * i + j)
            out[base : base + 16, :] = state[16 * j : 16 * (j + 1), :]
            out[base + 16 : base + 17, :] = g_mine * g_other


def k_scan(pieces, out):
    state = jnp.zeros((16, HEAD_DIM), F32)
    for i in range(32):
        out[i] = state
        state = state * pieces[17 * i + 16 : 17 * i + 17, :] + pieces[17 * i : 17 * i + 16, :]


def k_scan_back(pieces, factors, out):
    state = jnp.zeros((16, HEAD_DIM), F32)
    for i in reversed(range(32)):
        out[i] = state
        state = state * factors[17 * i + 16 : 17 * i + 17, :] + pieces[i]


def k_enter(core_ref, entering, mine, other, e_mine, e_send):
    first = core_ref[0] == 0
    for i in range(HALF):
        at = slice(i * 128, (i + 1) * 128)
        g0 = jnp.where(first, mine[512 + i : 513 + i, :], other[512 + i : 513 + i, :])
        s0 = jnp.where(first, mine[at, :], other[at, :])
        e0 = entering[at, :]
        e1 = e0 * g0 + s0
        e_mine[at, :] = jnp.where(first, e0, e1)
        e_send[at, :] = jnp.where(first, e1, e0)


def k_attend(
    core_ref, rows, q, k, v, within, e_mine, gate, gain, up,
    att_mine, dnormed, within_other, part, inward,
):
    core = core_ref[0]
    inward[...] = spread(inward_of(rows), 2)
    columns = spread(rows[HALF:8, :], 3)
    bias = biases(rows)
    squares = jnp.zeros((TOK, HEAD_DIM), F32)
    products = jnp.zeros((TOK, HEAD_DIM), F32)
    for slot in range(8):
        at = cols(core, slot)
        dn = up[:, at].astype(F32) * gain[:, at] * jax.nn.sigmoid(gate[:, at].astype(F32))
        dnormed[:, here(slot)] = dn
        if slot < HALF:
            carried = wide_dot(q[:, at], e_mine[slot * 128 : (slot + 1) * 128, :], 0)
            att = within[:, here(slot)] + carried * inward[:, here(slot)]
            att_mine[:, here(slot)] = att
            squares += att * att
            products += dn * att
        else:
            weight = weight_of(rows, columns[:, here(slot - HALF)], bias, slot)
            within_other[:, here(slot - HALF)] = mixed(weight, q[:, at], k[:, at], v[:, at])
    part[0] = squares
    part[1] = products


def k_sums(core_ref, q, within, inward, e_other, part, dnormed, att_other, sums):
    core = core_ref[0]
    squares, products = part[0], part[1]
    for i in range(HALF):
        slot = HALF + i
        carried = wide_dot(q[:, cols(core, slot)], e_other[i * 128 : (i + 1) * 128, :], 0)
        att = within[:, here(i)] + carried * inward[:, here(slot)]
        att_other[:, here(i)] = att
        squares += att * att
        products += dnormed[:, here(slot)] * att
    ones = jnp.ones((8, 2 * HEAD_DIM), BF16)
    line = lax.broadcasted_iota(jnp.int32, (8, TOK), 0)
    sums[...] = jnp.where(
        line < 4,
        dot(ones, jnp.concatenate(parts(squares, 2), axis=1), 1, 1),
        dot(ones, jnp.concatenate(parts(products, 2), axis=1), 1, 1),
    )


def k_mid(
    core_ref, rows, q, k, gate, att_mine, att_other, dnormed, inward,
    weights, turned, mixings, factor, scaled,
):
    core = core_ref[0]
    latest = latest_of(rows)
    columns = spread(rows[0:8, :], 3)
    biased = biases(rows)
    for slot in range(8):
        weights[slot] = weight_of(rows, columns[:, here(slot)], biased, slot)
    s = lax.broadcasted_iota(jnp.int32, (TOK, HEAD_DIM), 0)
    t = lax.broadcasted_iota(jnp.int32, (TOK, HEAD_DIM), 1)
    for part in range(2):
        at = here(part)
        kept = jnp.logical_and(s <= t + part * HEAD_DIM, s.astype(F32) >= latest[:, at])
        bias = jnp.where(kept, 0.0, NEG)
        for slot in range(8):
            turned[slot, :, at] = jnp.exp(rows[slot : slot + 1, at] - columns[:, here(slot)] + bias)
    for slot in reversed(range(8)):
        at = cols(core, slot)
        i = slot % HALF
        query = q[:, at]
        scaled[slot] = (query.astype(F32) * inward[:, here(slot)]).astype(BF16).T
        mixings[slot] = (turned[slot] * dot(k[:, at], query, 1, 1)).astype(BF16)
        att = (att_mine if slot < HALF else att_other)[:, here(i)]
        opening = jax.nn.sigmoid(gate[:, at].astype(F32))
        factor[:, here(slot)] = dnormed[:, here(slot)] * att * (1.0 - opening)


def grad_of(att, dnormed, inverse, projection):
    return ((dnormed - att * inverse * projection) * inverse).astype(BF16)


def k_grad(sums0, sums1, sums2, sums3, att, dnormed, scaled, grad, send, inverses, projections, *, features):
    total = sums0[...] + sums1[...] + sums2[...] + sums3[...]
    inverse = 1.0 / jnp.sqrt(total[0:1] / features + EPSILON)
    both = spread(jnp.concatenate([inverse, total[4:5] * inverse / features], axis=0), 3)
    inverse, projection = both[:, :HEAD_DIM], both[:, HEAD_DIM:]
    for i in range(HALF):
        slot = HALF + i
        value = grad_of(att[:, here(i)], dnormed[:, here(slot)], inverse, projection)
        grad[:, here(i)] = value
        send[i * 128 : (i + 1) * 128, :] = dot(scaled[slot], value, 1, 0)
    inverses[...] = inverse
    projections[...] = projection


def k_back(
    core_ref, inverses, projections, att_mine, dnormed, grad_other, k, v,
    weights, turned, factor, inward, scaled, e_mine, e_other,
    mine, grad_mine, gq, gate_out, mixed_back,
):
    core = core_ref[0]
    inverse, projection = inverses[...], projections[...]
    for slot in range(8):
        at = cols(core, slot)
        i = slot % HALF
        key, value = k[:, at], v[:, at]
        if slot < HALF:
            upstream = grad_of(att_mine[:, here(i)], dnormed[:, here(slot)], inverse, projection)
            grad_mine[:, here(i)] = upstream
            mine[i * 128 : (i + 1) * 128, :] = dot(scaled[slot], upstream, 1, 0)
        else:
            upstream = grad_other[:, here(i)]
        grad_mixing = (weights[slot] * dot(upstream, value, 1, 1)).astype(BF16)
        mixed_back[slot] = (turned[slot] * dot(value, upstream, 1, 1)).astype(BF16)
        state = (e_mine if slot < HALF else e_other)[i * 128 : (i + 1) * 128, :]
        carried = wide_dot(upstream, state, 1)
        gq[:, at] = (dot(grad_mixing, key, 1, 0) + carried * inward[:, here(slot)]).astype(BF16)
        gate_out[:, at] = (factor[:, here(slot)] * inverse).astype(BF16)


def k_pack_back(core_ref, mine, other, s_mine, s_other, out):
    first = core_ref[0] == 0
    for i in range(HALF):
        at = slice(i * 128, (i + 1) * 128)
        g0 = jnp.where(first, s_mine[512 + i : 513 + i, :], s_other[512 + i : 513 + i, :])
        b_mine, b_other = mine[at, :], other[at, :]
        state = jnp.where(first, b_mine + g0 * b_other, b_other + g0 * b_mine)
        for j in range(8):
            out[8 * i + j] = state[16 * j : 16 * (j + 1), :]


def k_leave(core_ref, leaving, mine, other, s_mine, s_other, l_mine, l_send):
    first = core_ref[0] == 0
    for i in range(HALF):
        at = slice(i * 128, (i + 1) * 128)
        g1 = jnp.where(first, s_other[512 + i : 513 + i, :], s_mine[512 + i : 513 + i, :])
        b1 = jnp.where(first, other[at, :], mine[at, :])
        l1 = leaving[at, :]
        l0 = l1 * g1 + b1
        l_mine[at, :] = jnp.where(first, l0, l1)
        l_send[at, :] = jnp.where(first, l1, l0)


def finish(state, scale, key, value, part_k, part_v):
    to_key = wide_dot(value, state, 1)
    to_value = wide_dot(key, state, 0)
    return (part_k + to_key * scale).astype(BF16), (part_v + to_value * scale).astype(BF16)


def k_end_mine(
    core_ref, rows, q, k, v, grad_mine, grad_other, mixed_back, mixings, l_mine, gq, gate_in,
    part_k, part_v, outward_other, k_mine, v_mine, out_q, out_gate, sems,
):
    core = core_ref[0]
    copies = fetch([(gq, out_q), (gate_in, out_gate)], sems)
    outward = spread(outward_of(rows, slice(0, 8)), 2)
    outward_other[...] = outward[:, 512:]
    for slot in range(8):
        i = slot % HALF
        at = cols(core, slot)
        upstream = (grad_mine if slot < HALF else grad_other)[:, here(i)]
        to_key = dot(mixed_back[slot], q[:, at], 1, 0)
        to_value = dot(mixings[slot], upstream, 1, 0)
        if slot < HALF:
            state = l_mine[i * 128 : (i + 1) * 128, :]
            k_mine[:, here(i)], v_mine[:, here(i)] = finish(
                state, outward[:, here(slot)], k[:, at], v[:, at], to_key, to_value
            )
        else:
            part_k[:, here(i)] = to_key
            part_v[:, here(i)] = to_value
    for copy in copies:
        copy.wait()


def k_end(
    core_ref, outward, k, v, part_k, part_v, l_other, k_mine, v_mine,
    out_k, out_v, kbuf, vbuf, sems,
):
    core = core_ref[0]
    there = half_cols(core)
    copies = fetch([(k_mine, out_k.at[:, there]), (v_mine, out_v.at[:, there])], sems)
    for i in range(HALF):
        slot = HALF + i
        at = cols(core, slot)
        state = l_other[i * 128 : (i + 1) * 128, :]
        kbuf[:, here(i)], vbuf[:, here(i)] = finish(
            state, outward[:, here(i)], k[:, at], v[:, at], part_k[:, here(i)], part_v[:, here(i)]
        )
        for n, (buf, out) in enumerate(((kbuf, out_k), (vbuf, out_v))):
            copies.append(pltpu.make_async_copy(buf.at[:, here(i)], out.at[:, at], sems.at[2 + 2 * i + n]))
            copies[-1].start()
    for copy in copies:
        copy.wait()


def local(q, k, v, decay, starts, gate, gain, up):
    places = lax.axis_size("seq")
    swap = [(i, i ^ 1) for i in range(places)]
    groups = [list(range(c, places, 2)) for c in range(2)]
    core = (lax.axis_index("seq") % 2).astype(jnp.int32).reshape(1)
    heads = lax.axis_size("head")
    features = q.shape[1] * heads
    gain = gain.reshape(1, -1)
    wide, half = (TOK, 1024), (TOK, 512)
    state, state_g = (512, HEAD_DIM), (520, HEAD_DIM)
    square = (8, TOK, TOK)
    buffer = pltpu.VMEM(half, BF16)

    def trade(a):
        return lax.all_to_all(a, "seq", 0, 0, axis_index_groups=groups)

    def around(a, step):
        return lax.ppermute(a, "head", [(i, (i + step) % heads) for i in range(heads)])

    begins = jnp.pad(starts.astype(F32), ((0, 7), (0, TOK - starts.shape[1])))
    aux = jnp.concatenate([decay, begins], axis=0)

    send, rows = call(
        k_first,
        [(state_g, F32), ((16, TOK), F32)],
        1, core, aux, k, v,
        hbm=(2, 3),
        vmem_mib=53.5,
        scratch=[buffer, buffer, pltpu.SemaphoreType.DMA((2,))],
    )
    s_other = lax.ppermute(send, "seq", swap)
    s_mine, within = call(
        k_local,
        [(state_g, F32), (half, F32)],
        1, core, rows, q, k, v,
        hbm=(2, 3, 4),
        vmem_mib=53,
        scratch=[buffer, buffer, buffer, pltpu.SemaphoreType.DMA((3,))],
    )
    (pieces,) = call(k_pack, [((544, HEAD_DIM), F32)], 1, core, s_mine, s_other)
    pieces = trade(pieces.reshape(32, 1, 17 * HEAD_DIM)).reshape(544, HEAD_DIM)
    (entering,) = call(k_scan, [((32, 16, HEAD_DIM), F32)], 0, pieces)
    entering = trade(entering).reshape(state)
    e_mine, e_send = call(k_enter, [(state, F32)] * 2, 1, core, entering, s_mine, s_other)
    e_other = lax.ppermute(e_send, "seq", swap)
    att_mine, dnormed, within_other, part, inward = call(
        k_attend,
        [(half, F32), (wide, F32), (half, F32), ((2, TOK, HEAD_DIM), F32), (wide, F32)],
        1, core, rows, q, k, v, within, e_mine, gate, gain, up,
    )
    att_other, sums = call(
        k_sums,
        [(half, F32), ((8, TOK), F32)],
        1, core, q, within_other, inward, e_other, part, dnormed,
    )
    others = [around(sums, step) for step in (2, 1, 3)]
    weights, turned, mixings, factor, scaled = call(
        k_mid,
        [(square, F32), (square, F32), (square, BF16), (wide, F32), ((8, HEAD_DIM, TOK), BF16)],
        1, core, rows, q, k, gate, att_mine, att_other, dnormed, inward,
        cost_estimate=pl.CostEstimate(flops=4_000_000_000, bytes_accessed=8_000_000, transcendentals=1_000_000),
    )
    grad_other, b_send, inverses, projections = call(
        functools.partial(k_grad, features=float(features)),
        [(half, BF16), (state, F32), ((TOK, HEAD_DIM), F32), ((TOK, HEAD_DIM), F32)],
        0, sums, *others, att_other, dnormed, scaled,
    )
    b_other = lax.ppermute(b_send, "seq", swap)
    b_mine, grad_mine, gq, grad_gate, mixed_back = call(
        k_back,
        [(state, F32), (half, BF16), (wide, BF16), (wide, BF16), (square, BF16)],
        1, core, inverses, projections, att_mine, dnormed, grad_other, k, v,
        weights, turned, factor, inward, scaled, e_mine, e_other,
    )
    (back,) = call(k_pack_back, [((32, 16, HEAD_DIM), F32)], 1, core, b_mine, b_other, s_mine, s_other)
    back = trade(back)
    (leaving,) = call(k_scan_back, [((32, 16, HEAD_DIM), F32)], 0, back, pieces)
    leaving = trade(leaving).reshape(state)
    l_mine, l_send = call(k_leave, [(state, F32)] * 2, 1, core, leaving, b_mine, b_other, s_mine, s_other)
    l_other = lax.ppermute(l_send, "seq", swap)
    part_k, part_v, outward, k_mine, v_mine, grad_query, grad_gate = call(
        k_end_mine,
        [(half, F32), (half, F32), (half, F32), (half, BF16), (half, BF16), (wide, BF16), (wide, BF16)],
        1, core, rows, q, k, v, grad_mine, grad_other, mixed_back, mixings, l_mine, gq, grad_gate,
        hbm_out=(5, 6),
        scratch=[pltpu.SemaphoreType.DMA((2,))],
    )
    grad_key, grad_value = call(
        k_end,
        [(wide, BF16), (wide, BF16)],
        1, core, outward, k, v, part_k, part_v, l_other, k_mine, v_mine,
        hbm_out=(0, 1),
        scratch=[buffer, buffer, pltpu.SemaphoreType.DMA((10,))],
    )
    return grad_query, grad_key, grad_value, grad_gate


def solution(mesh):
    token = P("seq", "head")
    return jax.shard_map(
        local,
        mesh=mesh,
        in_specs=(token, token, token, P("head", "seq"), P("seq", None), token, P("head"), token),
        out_specs=(token,) * 4,
        check_vma=False,
    )
```

time: 111 us -> 98.2 us (0.88)
  blocking collectives: 76.5 us -> 65.8 us
  starting transfers between devices: 12.5 us -> 16.7 us
  Pallas kernels: 16.6 us -> 12.7 us
  local copies, waits for them, and re-layouts: 3.86 us -> 0.03 us
  other arithmetic: 0 us -> 1.36 us
    all_to_all x1 -> x0, blocking collectives: 8.29 us -> none  [local(): sums = lax.all_to_all(sums, 'head', 0, 0)]
    ppermute x0 -> x3, starting transfers between devices: none -> 4.39 us  [around(): lax.ppermute(a, 'head', [(i, (i + step) % heads) for i in range(heads)])]
    pallas_call x14 -> x15, Pallas kernels: 16.6 us -> 12.7 us  [call(): pl.pallas_call(kernel, out_shape=[jax.ShapeDtypeStruct(s, d) for s, d in...]
    unnamed x22 -> x12, local copies, waits for them, and re-layouts: 3.86 us -> 0.03 us
    all_to_all x4, blocking collectives: 68.2 us -> 65.8 us  [trade(): return lax.all_to_all(a, 'seq', 0, 0, axis_index_groups=groups)]
  transfers between devices with their start and end apart: 4 -> 7, of which waited for: 2 -> 2; matrix products, arithmetic and copies ran while one was open for 0% -> 0% of each run, Pallas kernels for 8% -> 9%
where the time goes in v2:
time: 98.2 us; the launch traced here: 97.9 us
  blocking collectives  65.8 us (67%)
  starting transfers between devices  16.7 us (17%)
  Pallas kernels  12.7 us (13%)
  other arithmetic  1.36 us (1%)
    all_to_all x4, blocking collectives, trade(): return lax.all_to_all(a, 'seq', 0, 0, axis_index_groups=groups)  65.8 us
    pallas_call x15, Pallas kernels, call(): pl.pallas_call(kernel, out_shape=[jax.ShapeDtypeStruct(s, d) for s, d in...  12.7 us
    ppermute x3, starting transfers between devices, around(): lax.ppermute(a, 'head', [(i, (i + step) % heads) for i in range(heads)])  4.39 us
    ppermute x1, starting transfers between devices, local(): e_other = lax.ppermute(e_send, 'seq', swap)  3.71 us
    ppermute x1, starting transfers between devices, local(): l_other = lax.ppermute(l_send, 'seq', swap)  3.7 us
    ppermute x1, starting transfers between devices, local(): s_other = lax.ppermute(send, 'seq', swap)  3.33 us
  transfers between devices with their start and end apart: 7, of which 2 were waited for; matrix products, arithmetic and copies ran while one was open for 0% of the time, Pallas kernels for 9%

profile of v2, /device:TPU:1, one launch (start us, length us, event | category | flops | bytes accessed | tf_op | source)
XLA Modules:
  0.0 97.9 jit_solution(15201330365451416921)
XLA Ops:
  0.6 0.7 convert_element_type.5
  1.3 0.7 select_maximum_fusion.aux
  2.0 1.3 %shard_map.111 = (f32[520,128]{1,0:T(8,128)S(1)}, f32[16,256]{1,0:T(8,128)S(1)}) custom-call(s32[1]{0:T(128)} %bitcast.core_ref, f32[16,256]{1,0:T(8,128)S(1)} %select_maximum_fusion.aux, bf16[256,1024]{1,0:T(8,128)(2,1)} %k.13, bf16[256,1024]{1,0:T(8,128)(2,1)} %v.11), custom_call_target="tpu_custom_call" | custom-call | tf_op jit(solution)/shard_map/pallas_call | solution.py:39
  3.3 3.3 %collective-permute-start = (f32[520,128]{1,0:T(8,128)S(1)}, f32[520,128]{1,0:T(8,128)S(1)}, u32[]{:S(2)}, u32[]{:S(2)}) collective-permute-start(f32[520,128]{1,0:T(8,128)S(1)} %get-tuple-element.45), channel_id=1, source_target_pairs={{0,4},{4,0},{8,12},{12,8},{16,20},{20,16},{24,28},{28,24},{32,36},... | collective-permute-start | bytes 798728 | tf_op jit(solution)/shard_map/ppermute | solution.py:431
  6.7 0.0 copy-start
  6.7 0.0 copy-start.1
  6.7 0.0 copy-start.2
  6.7 0.0 copy-start.3
  6.7 0.0 copy-start.4
  6.7 0.0 copy-start.5
  6.7 2.0 %shard_map.112 = (f32[520,128]{1,0:T(8,128)S(1)}, f32[256,512]{1,0:T(8,128)S(1)}) custom-call(s32[1]{0:T(128)} %bitcast.core_ref, f32[16,256]{1,0:T(8,128)S(1)} %get-tuple-element.42.rows, bf16[256,1024]{1,0:T(8,128)(2,1)} %q.9, bf16[256,1024]{1,0:T(8,128)(2,1)} %k.13, bf16[256,1024]{1,0:T(8,128)(2,1)} %v.11), custom_call_target="tpu_custom_call" | custom-call | tf_op jit(solution)/shard_map/pallas_call | solution.py:39
  8.7 0.0 collective-permute-done.other.s_other
  8.7 0.1 shard_map.113
  8.8 19.5 %all_to_all.20 = f32[32,1,2176]{2,1,0:T(1,128)S(1)} all-to-all(f32[32,1,2176]{2,1,0:T(1,128)S(1)} %bitcast.8), channel_id=1, replica_groups={{0,8,16,24,32,40,48,56,64,72,80,88,96,104,112,120,128,136,144,152,160,1..., dimensions={0} | all-to-all | bytes 557056 | tf_op jit(solution)/shard_map/all_to_all | solution.py:415
  28.3 0.1 shard_map.114
  28.4 16.1 %all_to_all.21 = f32[32,16,128]{2,1,0:T(8,128)S(1)} all-to-all(f32[32,16,128]{2,1,0:T(8,128)S(1)} %shard_map.114), channel_id=1, replica_groups={{0,8,16,24,32,40,48,56,64,72,80,88,96,104,112,120,128,136,144,152,160,1..., dimensions={0} | all-to-all | bytes 524288 | tf_op jit(solution)/shard_map/all_to_all | solution.py:415
  44.5 0.1 shard_map.115
  44.6 3.7 %collective-permute-start.1 = (f32[512,128]{1,0:T(8,128)S(1)}, f32[512,128]{1,0:T(8,128)S(1)}, u32[]{:S(2)}, u32[]{:S(2)}) collective-permute-start(f32[512,128]{1,0:T(8,128)S(1)} %get-tuple-element.49), channel_id=1, source_target_pairs={{0,4},{4,0},{8,12},{12,8},{16,20},{20,16},{24,28},{28,24},{32,36},... | collective-permute-start | bytes 786440 | tf_op jit(solution)/shard_map/ppermute | solution.py:445
  48.3 0.0 copy-done
  48.3 0.0 copy-done.1
  48.3 0.0 copy-done.2
  48.3 0.0 copy-done.3
  48.3 0.0 copy-done.4
  48.3 0.0 copy-done.5
  48.3 1.5 %shard_map.116 = (f32[256,512]{1,0:T(8,128)S(1)}, f32[256,1024]{1,0:T(8,128)S(1)}, f32[256,512]{1,0:T(8,128)S(1)}, f32[2,256,128]{2,1,0:T(8,128)S(1)}, f32[256,1024]{1,0:T(8,128)S(1)}) custom-call(s32[1]{0:T(128)} %bitcast.core_ref, f32[16,256]{1,0:T(8,128)S(1)} %get-tuple-element.42.rows, bf16[256,1024]{1,0:T(8,128)(2,1)S(1)} %copy-done.2, ...), custom_call_target="tpu_custom_call" | custom-call | tf_op jit(solution)/shard_map/pallas_call | solution.py:39
  49.8 0.0 collective-permute-done.1.e_other
  49.8 0.5 shard_map.117
  50.2 2.7 %collective-permute-start.4 = (f32[8,256]{1,0:T(8,128)S(1)}, f32[8,256]{1,0:T(8,128)S(1)}, u32[]{:S(2)}, u32[]{:S(2)}) collective-permute-start(f32[8,256]{1,0:T(8,128)S(1)} %get-tuple-element.52.sums0), channel_id=1, source_target_pairs={{0,3},{1,0},{2,1},{3,2},{4,7},{5,4},{6,5},{7,6},{8,11},{9,8},{10,9... | collective-permute-start | bytes 24584 | tf_op jit(solution)/shard_map/ppermute | solution.py:418
  53.0 0.0 collective-permute-start.3
  53.0 1.6 %collective-permute-start.2 = (f32[8,256]{1,0:T(8,128)S(1)}, f32[8,256]{1,0:T(8,128)S(1)}, u32[]{:S(2)}, u32[]{:S(2)}) collective-permute-start(f32[8,256]{1,0:T(8,128)S(1)} %get-tuple-element.52.sums0), channel_id=1, source_target_pairs={{0,2},{1,3},{2,0},{3,1},{4,6},{5,7},{6,4},{7,5},{8,10},{9,11},{10,... | collective-permute-start | bytes 24584 | tf_op jit(solution)/shard_map/ppermute | solution.py:418
  54.6 1.9 %shard_map.118 = (f32[8,256,256]{2,1,0:T(8,128)S(1)}, f32[8,256,256]{2,1,0:T(8,128)S(1)}, bf16[8,256,256]{2,1,0:T(8,128)(2,1)S(1)}, f32[256,1024]{1,0:T(8,128)S(1)}, bf16[8,128,256]{2,1,0:T(8,128)(2,1)S(1)}) custom-call(s32[1]{0:T(128)} %bitcast.core_ref, f32[16,256]{1,0:T(8,128)S(1)} %get-tuple-element.42.rows, bf16[256,1024]{1,0:T(8,128)(2,1)S(1)} %copy-done.2, ...), custom_call_target="tpu_custom_call" | custom-call | flops 4000000000 | bytes 8000000 | tf_op jit(solution)/shard_map/pallas_call | solution.py:39
  56.5 0.0 collective-permute-done.4.sums3
  56.5 0.2 collective-permute-done.3.sums2
  56.7 0.3 collective-permute-done.2.sums1
  57.0 0.5 shard_map.119
  57.5 1.5 %collective-permute-start.5 = (f32[512,128]{1,0:T(8,128)S(1)}, f32[512,128]{1,0:T(8,128)S(1)}, u32[]{:S(2)}, u32[]{:S(2)}) collective-permute-start(f32[512,128]{1,0:T(8,128)S(1)} %get-tuple-element.66), channel_id=1, source_target_pairs={{0,4},{4,0},{8,12},{12,8},{16,20},{20,16},{24,28},{28,24},{32,36},... | collective-permute-start | bytes 786440 | tf_op jit(solution)/shard_map/ppermute | solution.py:468
  59.0 1.7 %shard_map.120 = (f32[512,128]{1,0:T(8,128)S(1)}, bf16[256,512]{1,0:T(8,128)(2,1)S(1)}, bf16[256,1024]{1,0:T(8,128)(2,1)S(1)}, bf16[256,1024]{1,0:T(8,128)(2,1)S(1)}, bf16[8,256,256]{2,1,0:T(8,128)(2,1)S(1)}) custom-call(s32[1]{0:T(128)} %bitcast.core_ref, f32[256,128]{1,0:T(8,128)S(1)} %get-tuple-element.56.inverses, ...), custom_call_target="tpu_custom_call" | custom-call | tf_op jit(solution)/shard_map/pallas_call | solution.py:39
  60.8 0.0 collective-permute-done.5.other
  60.8 0.1 shard_map.121
  60.8 14.3 %all_to_all.22.pieces = f32[32,16,128]{2,1,0:T(8,128)S(1)} all-to-all(f32[32,16,128]{2,1,0:T(8,128)S(1)} %shard_map.121), channel_id=1, replica_groups={{0,8,16,24,32,40,48,56,64,72,80,88,96,104,112,120,128,136,144,152,160,1..., dimensions={0} | all-to-all | bytes 524288 | tf_op jit(solution)/shard_map/all_to_all | solution.py:415
  75.1 0.1 shard_map.122
  75.2 15.9 %all_to_all.23 = f32[32,16,128]{2,1,0:T(8,128)S(1)} all-to-all(f32[32,16,128]{2,1,0:T(8,128)S(1)} %shard_map.122), channel_id=1, replica_groups={{0,8,16,24,32,40,48,56,64,72,80,88,96,104,112,120,128,136,144,152,160,1..., dimensions={0} | all-to-all | bytes 524288 | tf_op jit(solution)/shard_map/all_to_all | solution.py:415
  91.1 0.1 shard_map.123
  91.1 3.7 %collective-permute-start.6 = (f32[512,128]{1,0:T(8,128)S(1)}, f32[512,128]{1,0:T(8,128)S(1)}, u32[]{:S(2)}, u32[]{:S(2)}) collective-permute-start(f32[512,128]{1,0:T(8,128)S(1)} %get-tuple-element.74), channel_id=1, source_target_pairs={{0,4},{4,0},{8,12},{12,8},{16,20},{20,16},{24,28},{28,24},{32,36},... | collective-permute-start | bytes 786440 | tf_op jit(solution)/shard_map/ppermute | solution.py:480
  94.8 1.8 %shard_map.124 = (f32[256,512]{1,0:T(8,128)S(1)}, f32[256,512]{1,0:T(8,128)S(1)}, f32[256,512]{1,0:T(8,128)S(1)}, bf16[256,512]{1,0:T(8,128)(2,1)S(1)}, bf16[256...) custom-call(s32[1]{0:T(128)} %bitcast.core_ref, f32[16,256]{1,0:T(8,128)S(1)} %get-tuple-element.42.rows, ...), custom_call_target="tpu_custom_call" | custom-call | tf_op jit(solution)/shard_map/pallas_call | solution.py:39
  96.6 0.0 collective-permute-done.6.l_other
  96.6 1.2 %shard_map.125 = (bf16[256,1024]{1,0:T(8,128)(2,1)}, bf16[256,1024]{1,0:T(8,128)(2,1)}) custom-call(s32[1]{0:T(128)} %bitcast.core_ref, f32[256,512]{1,0:T(8,128)S(1)} %get-tuple-element.71.outward, bf16[256,1024]{1,0:T(8,128)(2,1)S(1)} %copy-done, bf16[256,1024]{1,0:T(8,128)(2,1)S(1)} %copy-done.1, f32[256,512]{1,0:T(8,128)S(1)} %get-tuple-element.72.part_k, ...), custom_call_target="tpu_custom_call" | custom-call | tf_op jit(solution)/shard_map/pallas_call | solution.py:39
Async XLA Ops:
  3.3 5.4 %collective-permute-start = (f32[520,128]{1,0:T(8,128)S(1)}, f32[520,128]{1,0:T(8,128)S(1)}, u32[]{:S(2)}, u32[]{:S(2)}) collective-permute-start(f32[520,128]{1,0:T(8,128)S(1)} %get-tuple-element.45), channel_id=1, source_target_pairs={{0,4},{4,0},{8,12},{12,8},{16,20},{20,16},{24,28},{28,24},{32,36},... | collective-permute-start | bytes 798728 | tf_op jit(solution)/shard_map/ppermute | solution.py:431
  6.7 41.6 %copy-start = (bf16[256,1024]{1,0:T(8,128)(2,1)S(1)}, bf16[256,1024]{1,0:T(8,128)(2,1)}, u32[]{:S(2)}) copy-start(bf16[256,1024]{1,0:T(8,128)(2,1)} %k.13) | copy-start | bytes 1572868
  6.7 41.6 %copy-start.1 = (bf16[256,1024]{1,0:T(8,128)(2,1)S(1)}, bf16[256,1024]{1,0:T(8,128)(2,1)}, u32[]{:S(2)}) copy-start(bf16[256,1024]{1,0:T(8,128)(2,1)} %v.11) | copy-start | bytes 1572868
  6.7 41.6 %copy-start.2 = (bf16[256,1024]{1,0:T(8,128)(2,1)S(1)}, bf16[256,1024]{1,0:T(8,128)(2,1)}, u32[]{:S(2)}) copy-start(bf16[256,1024]{1,0:T(8,128)(2,1)} %q.9) | copy-start | bytes 1572868
  6.7 41.6 %copy-start.3 = (bf16[256,1024]{1,0:T(8,128)(2,1)S(1)}, bf16[256,1024]{1,0:T(8,128)(2,1)}, u32[]{:S(2)}) copy-start(bf16[256,1024]{1,0:T(8,128)(2,1)} %up.1) | copy-start | bytes 1572868
  6.7 41.6 %copy-start.4 = (bf16[256,1024]{1,0:T(8,128)(2,1)S(1)}, bf16[256,1024]{1,0:T(8,128)(2,1)}, u32[]{:S(2)}) copy-start(bf16[256,1024]{1,0:T(8,128)(2,1)} %gate.3) | copy-start | bytes 1572868
  6.7 41.6 %copy-start.5 = (f32[1024]{0:T(1024)S(1)}, f32[1024]{0:T(1024)}, u32[]{:S(2)}) copy-start(f32[1024]{0:T(1024)} %param.14) | copy-start | bytes 12292
  44.6 5.2 %collective-permute-start.1 = (f32[512,128]{1,0:T(8,128)S(1)}, f32[512,128]{1,0:T(8,128)S(1)}, u32[]{:S(2)}, u32[]{:S(2)}) collective-permute-start(f32[512,128]{1,0:T(8,128)S(1)} %get-tuple-element.49), channel_id=1, source_target_pairs={{0,4},{4,0},{8,12},{12,8},{16,20},{20,16},{24,28},{28,24},{32,36},... | collective-permute-start | bytes 786440 | tf_op jit(solution)/shard_map/ppermute | solution.py:445
  50.2 6.3 %collective-permute-start.4 = (f32[8,256]{1,0:T(8,128)S(1)}, f32[8,256]{1,0:T(8,128)S(1)}, u32[]{:S(2)}, u32[]{:S(2)}) collective-permute-start(f32[8,256]{1,0:T(8,128)S(1)} %get-tuple-element.52.sums0), channel_id=1, source_target_pairs={{0,3},{1,0},{2,1},{3,2},{4,7},{5,4},{6,5},{7,6},{8,11},{9,8},{10,9... | collective-permute-start | bytes 24584 | tf_op jit(solution)/shard_map/ppermute | solution.py:418
  53.0 3.7 %collective-permute-start.3 = (f32[8,256]{1,0:T(8,128)S(1)}, f32[8,256]{1,0:T(8,128)S(1)}, u32[]{:S(2)}, u32[]{:S(2)}) collective-permute-start(f32[8,256]{1,0:T(8,128)S(1)} %get-tuple-element.52.sums0), channel_id=1, source_target_pairs={{0,1},{1,2},{2,3},{3,0},{4,5},{5,6},{6,7},{7,4},{8,9},{9,10},{10,1... | collective-permute-start | bytes 24584 | tf_op jit(solution)/shard_map/ppermute | solution.py:418
  53.0 4.0 %collective-permute-start.2 = (f32[8,256]{1,0:T(8,128)S(1)}, f32[8,256]{1,0:T(8,128)S(1)}, u32[]{:S(2)}, u32[]{:S(2)}) collective-permute-start(f32[8,256]{1,0:T(8,128)S(1)} %get-tuple-element.52.sums0), channel_id=1, source_target_pairs={{0,2},{1,3},{2,0},{3,1},{4,6},{5,7},{6,4},{7,5},{8,10},{9,11},{10,... | collective-permute-start | bytes 24584 | tf_op jit(solution)/shard_map/ppermute | solution.py:418
  57.5 3.2 %collective-permute-start.5 = (f32[512,128]{1,0:T(8,128)S(1)}, f32[512,128]{1,0:T(8,128)S(1)}, u32[]{:S(2)}, u32[]{:S(2)}) collective-permute-start(f32[512,128]{1,0:T(8,128)S(1)} %get-tuple-element.66), channel_id=1, source_target_pairs={{0,4},{4,0},{8,12},{12,8},{16,20},{20,16},{24,28},{28,24},{32,36},... | collective-permute-start | bytes 786440 | tf_op jit(solution)/shard_map/ppermute | solution.py:468
  91.1 5.5 %collective-permute-start.6 = (f32[512,128]{1,0:T(8,128)S(1)}, f32[512,128]{1,0:T(8,128)S(1)}, u32[]{:S(2)}, u32[]{:S(2)}) collective-permute-start(f32[512,128]{1,0:T(8,128)S(1)} %get-tuple-element.74), channel_id=1, source_target_pairs={{0,4},{4,0},{8,12},{12,8},{16,20},{20,16},{24,28},{28,24},{32,36},... | collective-permute-start | bytes 786440 | tf_op jit(solution)/shard_map/ppermute | solution.py:480

commit v3 on v2

--- a/solution.py
+++ b/solution.py
@@ -32,17 +32,18 @@
     return dot(jnp.concatenate([a, a], axis=1), jnp.concatenate(parts(state, 2), axis=axis), 1, axis)
 
 
-def call(kernel, outs, n_smem, *args, hbm=(), hbm_out=(), scratch=(), vmem_mib=24, **kw):
+def call(kernel, outs, n_smem, *args, hbm=(), hbm_out=(), scratch=(), **kw):
     smem = pl.BlockSpec(memory_space=pltpu.SMEM)
     vmem = pl.BlockSpec(memory_space=pltpu.VMEM)
     far = pl.BlockSpec(memory_space=pltpu.HBM)
+    args = [pltpu.with_memory_space_constraint(a, pltpu.HBM) if n in hbm else a for n, a in enumerate(args)]
     return pl.pallas_call(
         kernel,
         out_shape=[jax.ShapeDtypeStruct(s, d) for s, d in outs],
         in_specs=[smem] * n_smem + [far if n in hbm else vmem for n in range(n_smem, len(args))],
         out_specs=[far if n in hbm_out else vmem for n in range(len(outs))],
         scratch_shapes=list(scratch),
-        compiler_params=pltpu.CompilerParams(vmem_limit_bytes=int(vmem_mib * 1024 * 1024)),
+        compiler_params=pltpu.CompilerParams(vmem_limit_bytes=24 * 1024 * 1024),
         **kw,
     )(*args)
 
@@ -100,29 +101,42 @@
     return copies
 
 
-def k_first(core_ref, aux, k, v, send, rows, kbuf, vbuf, sems):
+def k_first(
+    core_ref, starts_in, decay, q, k, v, send, rows, q_mine, k_mine, v_mine, kbuf, vbuf, dbuf, starts, sems
+):
     core = core_ref[0]
     there = half_cols(1 - core)
-    copies = fetch([(k.at[:, there], kbuf), (v.at[:, there], vbuf)], sems)
+    mine = half_cols(core)
+    copies = fetch(
+        [
+            (decay, dbuf), (starts_in, starts), (k.at[:, there], kbuf), (v.at[:, there], vbuf),
+            (k.at[:, mine], k_mine), (v.at[:, mine], v_mine), (q.at[:, mine], q_mine),
+        ],
+        sems,
+    )
     a = lax.broadcasted_iota(jnp.int32, (TOK, TOK), 0)
     b = lax.broadcasted_iota(jnp.int32, (TOK, TOK), 1)
-    d = aux[0:8, :]
+    copies[0].wait()
+    d = dbuf[...]
     d = jnp.where(core == 0, d, jnp.concatenate([d[HALF:], d[:HALF]], axis=0))
     sums = dot(jnp.concatenate(parts(d, 3), axis=0), (a <= b).astype(BF16), 1, 0)
     rows[0:8, :] = sums[0:8] + sums[8:16] + sums[16:24]
-    place = lax.broadcasted_iota(jnp.int32, (1, TOK), 1).astype(F32)
-    latest = jnp.full((1, TOK), -1.0, F32)
+    copies[1].wait()
+    place = lax.broadcasted_iota(jnp.int32, (8, TOK), 1)
+    latest = jnp.full((8, TOK), -1, jnp.int32)
     for j in range(4):
-        begin = aux[8:9, j : j + 1]
-        latest = jnp.maximum(latest, jnp.where(begin <= place, begin, -1.0))
-    rows[8:16, :] = jnp.broadcast_to(latest, (8, TOK))
+        begin = starts[0, j]
+        latest = jnp.maximum(latest, jnp.where(begin <= place, begin, -1))
+    rows[8:16, :] = latest.astype(F32)
     outward = spread(outward_of(rows, slice(HALF, 8)), 2)
     through = through_of(rows)
     send[512:520, :] = jnp.concatenate([through[HALF:8], through[0:HALF]], axis=0)
-    for copy in copies:
+    copies[2].wait()
+    copies[3].wait()
+    for i in range(HALF):
+        send[i * 128 : (i + 1) * 128, :] = state_of(kbuf[:, here(i)], outward[:, here(i)], vbuf[:, here(i)])
+    for copy in copies[4:]:
         copy.wait()
-    for i in range(HALF):
-        send[i * 128 : (i + 1) * 128, :] = state_of(kbuf[:, here(i)], outward[:, here(i)], vbuf[:, here(i)])
 
 
 def mixed(weight, query, key, value):
@@ -147,22 +161,16 @@
     )
 
 
-def k_local(core_ref, rows, q, k, v, mine, within, qbuf, kbuf, vbuf, sems):
-    core = core_ref[0]
-    there = half_cols(core)
-    copies = fetch([(k.at[:, there], kbuf), (v.at[:, there], vbuf), (q.at[:, there], qbuf)], sems)
+def k_local(rows, q, k, v, mine, within):
     columns = spread(rows[0:HALF, :], 3)
     bias = biases(rows)
     outward = spread(outward_of(rows, slice(0, HALF)), 2)
     mine[512:520, :] = through_of(rows)
-    copies[0].wait()
-    copies[1].wait()
-    for i in range(HALF):
-        mine[i * 128 : (i + 1) * 128, :] = state_of(kbuf[:, here(i)], outward[:, here(i)], vbuf[:, here(i)])
-    copies[2].wait()
+    for i in range(HALF):
+        mine[i * 128 : (i + 1) * 128, :] = state_of(k[:, here(i)], outward[:, here(i)], v[:, here(i)])
     for i in range(HALF):
         weight = weight_of(rows, columns[:, here(i)], bias, i)
-        within[:, here(i)] = mixed(weight, qbuf[:, here(i)], kbuf[:, here(i)], vbuf[:, here(i)])
+        within[:, here(i)] = mixed(weight, q[:, here(i)], k[:, here(i)], v[:, here(i)])
 
 
 def k_pack(core_ref, mine, other, out):
@@ -417,25 +425,20 @@
     def around(a, step):
         return lax.ppermute(a, "head", [(i, (i + step) % heads) for i in range(heads)])
 
-    begins = jnp.pad(starts.astype(F32), ((0, 7), (0, TOK - starts.shape[1])))
-    aux = jnp.concatenate([decay, begins], axis=0)
-
-    send, rows = call(
+    send, rows, *own = call(
         k_first,
-        [(state_g, F32), ((16, TOK), F32)],
-        1, core, aux, k, v,
-        hbm=(2, 3),
-        vmem_mib=53.5,
-        scratch=[buffer, buffer, pltpu.SemaphoreType.DMA((2,))],
+        [(state_g, F32), ((16, TOK), F32)] + [(half, BF16)] * 3,
+        1, core, starts, decay, q, k, v,
+        hbm=(1, 2, 3, 4, 5),
+        scratch=[
+            buffer, buffer, pltpu.VMEM((8, TOK), F32), pltpu.SMEM((1, 4), jnp.int32), pltpu.SemaphoreType.DMA((7,)),
+        ],
     )
     s_other = lax.ppermute(send, "seq", swap)
     s_mine, within = call(
         k_local,
         [(state_g, F32), (half, F32)],
-        1, core, rows, q, k, v,
-        hbm=(2, 3, 4),
-        vmem_mib=53,
-        scratch=[buffer, buffer, buffer, pltpu.SemaphoreType.DMA((3,))],
+        0, rows, *own,
     )
     (pieces,) = call(k_pack, [((544, HEAD_DIM), F32)], 1, core, s_mine, s_other)
     pieces = trade(pieces.reshape(32, 1, 17 * HEAD_DIM)).reshape(544, HEAD_DIM)

time: 98.2 us -> 96.2 us (0.980)
  other arithmetic: 1.36 us -> 0 us
  transfers between devices with their start and end apart: 7 -> 7, of which waited for: 2 -> 3; matrix products, arithmetic and copies ran while one was open for 0% -> 0% of each run, Pallas kernels for 9% -> 8%
where the time goes in v3:
time: 96.2 us; the launch traced here: 95.9 us
  blocking collectives  65.6 us (68%)
  starting transfers between devices  16.7 us (17%)
  Pallas kernels  12 us (12%)
  between operations  0.97 us (1%)
    all_to_all x4, blocking collectives, trade(): return lax.all_to_all(a, 'seq', 0, 0, axis_index_groups=groups)  65.6 us
    pallas_call x15, Pallas kernels, call(): pl.pallas_call(kernel, out_shape=[jax.ShapeDtypeStruct(s, d) for s, d in...  12 us
    ppermute x3, starting transfers between devices, around(): lax.ppermute(a, 'head', [(i, (i + step) % heads) for i in range(heads)])  4.39 us
    ppermute x1, starting transfers between devices, local(): l_other = lax.ppermute(l_send, 'seq', swap)  3.7 us
    ppermute x1, starting transfers between devices, local(): e_other = lax.ppermute(e_send, 'seq', swap)  3.69 us
    ppermute x1, starting transfers between devices, local(): s_other = lax.ppermute(send, 'seq', swap)  3.33 us
  transfers between devices with their start and end apart: 7, of which 3 were waited for; matrix products, arithmetic and copies ran while one was open for 0% of the time, Pallas kernels for 8%

profile of v3, /device:TPU:1, one launch (start us, length us, event | category | flops | bytes accessed | tf_op | source)
XLA Modules:
  0.0 95.9 jit_solution(12134487639670012875)
XLA Ops:
  0.6 1.6 %shard_map.111 = (f32[520,128]{1,0:T(8,128)S(1)}, f32[16,256]{1,0:T(8,128)S(1)}, bf16[256,512]{1,0:T(8,128)(2,1)S(1)}, bf16[256,512]{1,0:T(8,128)(2,1)S(1)}, bf16[256,512]{1,0:T(8,128)(2,1)S(1)}) custom-call(s32[1]{0:T(128)} %bitcast.core_ref, s32[1,4]{1,0:T(1,128)} %starts_in.1, f32[8,256]{1,0:T(8,128)} %decay.1, bf16[256,1024]{1,0:T(8,128)(2,1)} %q.9, ...), custom_call_target="tpu_custom_call" | custom-call | tf_op jit(solution)/shard_map/pallas_call | solution.py:40
  2.2 0.0 copy-start
  2.2 0.0 copy-start.1
  2.2 0.0 copy-start.2
  2.3 0.0 copy-start.3
  2.3 0.0 copy-start.4
  2.3 0.0 copy-start.5
  2.3 3.3 %collective-permute-start = (f32[520,128]{1,0:T(8,128)S(1)}, f32[520,128]{1,0:T(8,128)S(1)}, u32[]{:S(2)}, u32[]{:S(2)}) collective-permute-start(f32[520,128]{1,0:T(8,128)S(1)} %get-tuple-element.51), channel_id=1, source_target_pairs={{0,4},{4,0},{8,12},{12,8},{16,20},{20,16},{24,28},{28,24},{32,36},... | collective-permute-start | bytes 798728 | tf_op jit(solution)/shard_map/ppermute | solution.py:437
  5.6 1.0 %shard_map.112 = (f32[520,128]{1,0:T(8,128)S(1)}, f32[256,512]{1,0:T(8,128)S(1)}) custom-call(f32[16,256]{1,0:T(8,128)S(1)} %get-tuple-element.45.rows, bf16[256,512]{1,0:T(8,128)(2,1)S(1)} %get-tuple-element.46.q, bf16[256,512]{1,0:T(8,128)(2,1)S(1)} %get-tuple-element.47.k, bf16[256,512]{1,0:T(8,128)(2,1)S(1)} %get-tuple-element.48.v), custom_call_target="tpu_custom_call" | custom-call | tf_op jit(solution)/shard_map/pallas_call | solution.py:40
  6.7 0.1 collective-permute-done.other.s_other
  6.8 0.1 shard_map.113
  6.8 18.8 %all_to_all.20 = f32[32,1,2176]{2,1,0:T(1,128)S(1)} all-to-all(f32[32,1,2176]{2,1,0:T(1,128)S(1)} %bitcast.8), channel_id=1, replica_groups={{0,8,16,24,32,40,48,56,64,72,80,88,96,104,112,120,128,136,144,152,160,1..., dimensions={0} | all-to-all | bytes 557056 | tf_op jit(solution)/shard_map/all_to_all | solution.py:423
  25.7 0.1 shard_map.114
  25.8 16.6 %all_to_all.21 = f32[32,16,128]{2,1,0:T(8,128)S(1)} all-to-all(f32[32,16,128]{2,1,0:T(8,128)S(1)} %shard_map.114), channel_id=1, replica_groups={{0,8,16,24,32,40,48,56,64,72,80,88,96,104,112,120,128,136,144,152,160,1..., dimensions={0} | all-to-all | bytes 524288 | tf_op jit(solution)/shard_map/all_to_all | solution.py:423
  42.4 0.1 shard_map.115
  42.4 3.7 %collective-permute-start.1 = (f32[512,128]{1,0:T(8,128)S(1)}, f32[512,128]{1,0:T(8,128)S(1)}, u32[]{:S(2)}, u32[]{:S(2)}) collective-permute-start(f32[512,128]{1,0:T(8,128)S(1)} %get-tuple-element.55), channel_id=1, source_target_pairs={{0,4},{4,0},{8,12},{12,8},{16,20},{20,16},{24,28},{28,24},{32,36},... | collective-permute-start | bytes 786440 | tf_op jit(solution)/shard_map/ppermute | solution.py:448
  46.1 0.0 copy-done
  46.1 0.0 copy-done.1
  46.1 0.0 copy-done.2
  46.1 0.0 copy-done.3
  46.1 0.0 copy-done.4
  46.2 0.0 copy-done.5
  46.2 1.5 %shard_map.116 = (f32[256,512]{1,0:T(8,128)S(1)}, f32[256,1024]{1,0:T(8,128)S(1)}, f32[256,512]{1,0:T(8,128)S(1)}, f32[2,256,128]{2,1,0:T(8,128)S(1)}, f32[256,1024]{1,0:T(8,128)S(1)}) custom-call(s32[1]{0:T(128)} %bitcast.core_ref, f32[16,256]{1,0:T(8,128)S(1)} %get-tuple-element.45.rows, bf16[256,1024]{1,0:T(8,128)(2,1)S(1)} %copy-done.2, ...), custom_call_target="tpu_custom_call" | custom-call | tf_op jit(solution)/shard_map/pallas_call | solution.py:40
  47.6 0.0 collective-permute-done.1.e_other
  47.6 0.4 shard_map.117
  48.1 2.7 %collective-permute-start.4 = (f32[8,256]{1,0:T(8,128)S(1)}, f32[8,256]{1,0:T(8,128)S(1)}, u32[]{:S(2)}, u32[]{:S(2)}) collective-permute-start(f32[8,256]{1,0:T(8,128)S(1)} %get-tuple-element.58.sums0), channel_id=1, source_target_pairs={{0,3},{1,0},{2,1},{3,2},{4,7},{5,4},{6,5},{7,6},{8,11},{9,8},{10,9... | collective-permute-start | bytes 24584 | tf_op jit(solution)/shard_map/ppermute | solution.py:426
  50.8 0.0 collective-permute-start.3
  50.8 1.6 %collective-permute-start.2 = (f32[8,256]{1,0:T(8,128)S(1)}, f32[8,256]{1,0:T(8,128)S(1)}, u32[]{:S(2)}, u32[]{:S(2)}) collective-permute-start(f32[8,256]{1,0:T(8,128)S(1)} %get-tuple-element.58.sums0), channel_id=1, source_target_pairs={{0,2},{1,3},{2,0},{3,1},{4,6},{5,7},{6,4},{7,5},{8,10},{9,11},{10,... | collective-permute-start | bytes 24584 | tf_op jit(solution)/shard_map/ppermute | solution.py:426
  52.5 1.9 %shard_map.118 = (f32[8,256,256]{2,1,0:T(8,128)S(1)}, f32[8,256,256]{2,1,0:T(8,128)S(1)}, bf16[8,256,256]{2,1,0:T(8,128)(2,1)S(1)}, f32[256,1024]{1,0:T(8,128)S(1)}, bf16[8,128,256]{2,1,0:T(8,128)(2,1)S(1)}) custom-call(s32[1]{0:T(128)} %bitcast.core_ref, f32[16,256]{1,0:T(8,128)S(1)} %get-tuple-element.45.rows, bf16[256,1024]{1,0:T(8,128)(2,1)S(1)} %copy-done.2, ...), custom_call_target="tpu_custom_call" | custom-call | flops 4000000000 | bytes 8000000 | tf_op jit(solution)/shard_map/pallas_call | solution.py:40
  54.4 0.0 collective-permute-done.4.sums3
  54.4 0.2 collective-permute-done.3.sums2
  54.5 0.3 collective-permute-done.2.sums1
  54.8 0.5 shard_map.119
  55.4 1.5 %collective-permute-start.5 = (f32[512,128]{1,0:T(8,128)S(1)}, f32[512,128]{1,0:T(8,128)S(1)}, u32[]{:S(2)}, u32[]{:S(2)}) collective-permute-start(f32[512,128]{1,0:T(8,128)S(1)} %get-tuple-element.72), channel_id=1, source_target_pairs={{0,4},{4,0},{8,12},{12,8},{16,20},{20,16},{24,28},{28,24},{32,36},... | collective-permute-start | bytes 786440 | tf_op jit(solution)/shard_map/ppermute | solution.py:471
  56.9 1.8 %shard_map.120 = (f32[512,128]{1,0:T(8,128)S(1)}, bf16[256,512]{1,0:T(8,128)(2,1)S(1)}, bf16[256,1024]{1,0:T(8,128)(2,1)S(1)}, bf16[256,1024]{1,0:T(8,128)(2,1)S(1)}, bf16[8,256,256]{2,1,0:T(8,128)(2,1)S(1)}) custom-call(s32[1]{0:T(128)} %bitcast.core_ref, f32[256,128]{1,0:T(8,128)S(1)} %get-tuple-element.62.inverses, ...), custom_call_target="tpu_custom_call" | custom-call | tf_op jit(solution)/shard_map/pallas_call | solution.py:40
  58.7 0.0 collective-permute-done.5.other
  58.7 0.1 shard_map.121
  58.7 14.4 %all_to_all.22.pieces = f32[32,16,128]{2,1,0:T(8,128)S(1)} all-to-all(f32[32,16,128]{2,1,0:T(8,128)S(1)} %shard_map.121), channel_id=1, replica_groups={{0,8,16,24,32,40,48,56,64,72,80,88,96,104,112,120,128,136,144,152,160,1..., dimensions={0} | all-to-all | bytes 524288 | tf_op jit(solution)/shard_map/all_to_all | solution.py:423
  73.1 0.1 shard_map.122
  73.2 15.8 %all_to_all.23 = f32[32,16,128]{2,1,0:T(8,128)S(1)} all-to-all(f32[32,16,128]{2,1,0:T(8,128)S(1)} %shard_map.122), channel_id=1, replica_groups={{0,8,16,24,32,40,48,56,64,72,80,88,96,104,112,120,128,136,144,152,160,1..., dimensions={0} | all-to-all | bytes 524288 | tf_op jit(solution)/shard_map/all_to_all | solution.py:423
  89.0 0.1 shard_map.123
  89.0 3.7 %collective-permute-start.6 = (f32[512,128]{1,0:T(8,128)S(1)}, f32[512,128]{1,0:T(8,128)S(1)}, u32[]{:S(2)}, u32[]{:S(2)}) collective-permute-start(f32[512,128]{1,0:T(8,128)S(1)} %get-tuple-element.80), channel_id=1, source_target_pairs={{0,4},{4,0},{8,12},{12,8},{16,20},{20,16},{24,28},{28,24},{32,36},... | collective-permute-start | bytes 786440 | tf_op jit(solution)/shard_map/ppermute | solution.py:483
  92.7 1.8 %shard_map.124 = (f32[256,512]{1,0:T(8,128)S(1)}, f32[256,512]{1,0:T(8,128)S(1)}, f32[256,512]{1,0:T(8,128)S(1)}, bf16[256,512]{1,0:T(8,128)(2,1)S(1)}, bf16[256...) custom-call(s32[1]{0:T(128)} %bitcast.core_ref, f32[16,256]{1,0:T(8,128)S(1)} %get-tuple-element.45.rows, ...), custom_call_target="tpu_custom_call" | custom-call | tf_op jit(solution)/shard_map/pallas_call | solution.py:40
  94.5 0.0 collective-permute-done.6.l_other
  94.5 1.2 %shard_map.125 = (bf16[256,1024]{1,0:T(8,128)(2,1)}, bf16[256,1024]{1,0:T(8,128)(2,1)}) custom-call(s32[1]{0:T(128)} %bitcast.core_ref, f32[256,512]{1,0:T(8,128)S(1)} %get-tuple-element.77.outward, bf16[256,1024]{1,0:T(8,128)(2,1)S(1)} %copy-done, bf16[256,1024]{1,0:T(8,128)(2,1)S(1)} %copy-done.1, f32[256,512]{1,0:T(8,128)S(1)} %get-tuple-element.78.part_k, ...), custom_call_target="tpu_custom_call" | custom-call | tf_op jit(solution)/shard_map/pallas_call | solution.py:40
Async XLA Ops:
  2.2 43.9 %copy-start = (bf16[256,1024]{1,0:T(8,128)(2,1)S(1)}, bf16[256,1024]{1,0:T(8,128)(2,1)}, u32[]{:S(2)}) copy-start(bf16[256,1024]{1,0:T(8,128)(2,1)} %k.11) | copy-start | bytes 1572868
  2.2 43.9 %copy-start.1 = (bf16[256,1024]{1,0:T(8,128)(2,1)S(1)}, bf16[256,1024]{1,0:T(8,128)(2,1)}, u32[]{:S(2)}) copy-start(bf16[256,1024]{1,0:T(8,128)(2,1)} %v.9) | copy-start | bytes 1572868
  2.2 43.9 %copy-start.2 = (bf16[256,1024]{1,0:T(8,128)(2,1)S(1)}, bf16[256,1024]{1,0:T(8,128)(2,1)}, u32[]{:S(2)}) copy-start(bf16[256,1024]{1,0:T(8,128)(2,1)} %q.9) | copy-start | bytes 1572868
  2.3 43.9 %copy-start.3 = (bf16[256,1024]{1,0:T(8,128)(2,1)S(1)}, bf16[256,1024]{1,0:T(8,128)(2,1)}, u32[]{:S(2)}) copy-start(bf16[256,1024]{1,0:T(8,128)(2,1)} %up.1) | copy-start | bytes 1572868
  2.3 43.9 %copy-start.4 = (bf16[256,1024]{1,0:T(8,128)(2,1)S(1)}, bf16[256,1024]{1,0:T(8,128)(2,1)}, u32[]{:S(2)}) copy-start(bf16[256,1024]{1,0:T(8,128)(2,1)} %gate.3) | copy-start | bytes 1572868
  2.3 43.9 %copy-start.5 = (f32[1024]{0:T(1024)S(1)}, f32[1024]{0:T(1024)}, u32[]{:S(2)}) copy-start(f32[1024]{0:T(1024)} %param.14) | copy-start | bytes 12292
  2.3 4.5 %collective-permute-start = (f32[520,128]{1,0:T(8,128)S(1)}, f32[520,128]{1,0:T(8,128)S(1)}, u32[]{:S(2)}, u32[]{:S(2)}) collective-permute-start(f32[520,128]{1,0:T(8,128)S(1)} %get-tuple-element.51), channel_id=1, source_target_pairs={{0,4},{4,0},{8,12},{12,8},{16,20},{20,16},{24,28},{28,24},{32,36},... | collective-permute-start | bytes 798728 | tf_op jit(solution)/shard_map/ppermute | solution.py:437
  42.4 5.2 %collective-permute-start.1 = (f32[512,128]{1,0:T(8,128)S(1)}, f32[512,128]{1,0:T(8,128)S(1)}, u32[]{:S(2)}, u32[]{:S(2)}) collective-permute-start(f32[512,128]{1,0:T(8,128)S(1)} %get-tuple-element.55), channel_id=1, source_target_pairs={{0,4},{4,0},{8,12},{12,8},{16,20},{20,16},{24,28},{28,24},{32,36},... | collective-permute-start | bytes 786440 | tf_op jit(solution)/shard_map/ppermute | solution.py:448
  48.1 6.3 %collective-permute-start.4 = (f32[8,256]{1,0:T(8,128)S(1)}, f32[8,256]{1,0:T(8,128)S(1)}, u32[]{:S(2)}, u32[]{:S(2)}) collective-permute-start(f32[8,256]{1,0:T(8,128)S(1)} %get-tuple-element.58.sums0), channel_id=1, source_target_pairs={{0,3},{1,0},{2,1},{3,2},{4,7},{5,4},{6,5},{7,6},{8,11},{9,8},{10,9... | collective-permute-start | bytes 24584 | tf_op jit(solution)/shard_map/ppermute | solution.py:426
  50.8 3.7 %collective-permute-start.3 = (f32[8,256]{1,0:T(8,128)S(1)}, f32[8,256]{1,0:T(8,128)S(1)}, u32[]{:S(2)}, u32[]{:S(2)}) collective-permute-start(f32[8,256]{1,0:T(8,128)S(1)} %get-tuple-element.58.sums0), channel_id=1, source_target_pairs={{0,1},{1,2},{2,3},{3,0},{4,5},{5,6},{6,7},{7,4},{8,9},{9,10},{10,1... | collective-permute-start | bytes 24584 | tf_op jit(solution)/shard_map/ppermute | solution.py:426
  50.8 4.0 %collective-permute-start.2 = (f32[8,256]{1,0:T(8,128)S(1)}, f32[8,256]{1,0:T(8,128)S(1)}, u32[]{:S(2)}, u32[]{:S(2)}) collective-permute-start(f32[8,256]{1,0:T(8,128)S(1)} %get-tuple-element.58.sums0), channel_id=1, source_target_pairs={{0,2},{1,3},{2,0},{3,1},{4,6},{5,7},{6,4},{7,5},{8,10},{9,11},{10,... | collective-permute-start | bytes 24584 | tf_op jit(solution)/shard_map/ppermute | solution.py:426
  55.4 3.3 %collective-permute-start.5 = (f32[512,128]{1,0:T(8,128)S(1)}, f32[512,128]{1,0:T(8,128)S(1)}, u32[]{:S(2)}, u32[]{:S(2)}) collective-permute-start(f32[512,128]{1,0:T(8,128)S(1)} %get-tuple-element.72), channel_id=1, source_target_pairs={{0,4},{4,0},{8,12},{12,8},{16,20},{20,16},{24,28},{28,24},{32,36},... | collective-permute-start | bytes 786440 | tf_op jit(solution)/shard_map/ppermute | solution.py:471
  89.0 5.5 %collective-permute-start.6 = (f32[512,128]{1,0:T(8,128)S(1)}, f32[512,128]{1,0:T(8,128)S(1)}, u32[]{:S(2)}, u32[]{:S(2)}) collective-permute-start(f32[512,128]{1,0:T(8,128)S(1)} %get-tuple-element.80), channel_id=1, source_target_pairs={{0,4},{4,0},{8,12},{12,8},{16,20},{20,16},{24,28},{28,24},{32,36},... | collective-permute-start | bytes 786440 | tf_op jit(solution)/shard_map/ppermute | solution.py:483

commit v4 on v3

--- a/solution.py
+++ b/solution.py
@@ -90,8 +90,8 @@
     return jnp.broadcast_to(jnp.exp(last), (8, HEAD_DIM))
 
 
-def state_of(left, scale, right):
-    return dot((left.astype(F32) * scale).astype(BF16), right, 0, 0)
+def turn(left, line):
+    return (left.T.astype(F32) * line).astype(BF16)
 
 
 def fetch(pairs, sems):
@@ -128,13 +128,14 @@
         begin = starts[0, j]
         latest = jnp.maximum(latest, jnp.where(begin <= place, begin, -1))
     rows[8:16, :] = latest.astype(F32)
-    outward = spread(outward_of(rows, slice(HALF, 8)), 2)
+    outward = outward_of(rows, slice(HALF, 8))
     through = through_of(rows)
     send[512:520, :] = jnp.concatenate([through[HALF:8], through[0:HALF]], axis=0)
     copies[2].wait()
     copies[3].wait()
     for i in range(HALF):
-        send[i * 128 : (i + 1) * 128, :] = state_of(kbuf[:, here(i)], outward[:, here(i)], vbuf[:, here(i)])
+        turned = turn(kbuf[:, here(i)], outward[i : i + 1, :])
+        send[i * 128 : (i + 1) * 128, :] = dot(turned, vbuf[:, here(i)], 1, 0)
     for copy in copies[4:]:
         copy.wait()
 
@@ -161,13 +162,16 @@
     )
 
 
-def k_local(rows, q, k, v, mine, within):
-    columns = spread(rows[0:HALF, :], 3)
+def k_local(rows, q, k, v, mine, within, summed, inward):
+    inward[...] = spread(inward_of(rows), 2)
+    columns = spread(rows[0:8, :], 3)
+    summed[...] = columns
     bias = biases(rows)
-    outward = spread(outward_of(rows, slice(0, HALF)), 2)
+    outward = outward_of(rows, slice(0, HALF))
     mine[512:520, :] = through_of(rows)
     for i in range(HALF):
-        mine[i * 128 : (i + 1) * 128, :] = state_of(k[:, here(i)], outward[:, here(i)], v[:, here(i)])
+        turned = turn(k[:, here(i)], outward[i : i + 1, :])
+        mine[i * 128 : (i + 1) * 128, :] = dot(turned, v[:, here(i)], 1, 0)
     for i in range(HALF):
         weight = weight_of(rows, columns[:, here(i)], bias, i)
         within[:, here(i)] = mixed(weight, q[:, here(i)], k[:, here(i)], v[:, here(i)])
@@ -213,12 +217,10 @@
 
 
 def k_attend(
-    core_ref, rows, q, k, v, within, e_mine, gate, gain, up,
-    att_mine, dnormed, within_other, part, inward,
+    core_ref, rows, summed, q, k, v, within, inward, e_mine, gate, gain, up,
+    att_mine, dnormed, within_other, part,
 ):
     core = core_ref[0]
-    inward[...] = spread(inward_of(rows), 2)
-    columns = spread(rows[HALF:8, :], 3)
     bias = biases(rows)
     squares = jnp.zeros((TOK, HEAD_DIM), F32)
     products = jnp.zeros((TOK, HEAD_DIM), F32)
@@ -233,7 +235,7 @@
             squares += att * att
             products += dn * att
         else:
-            weight = weight_of(rows, columns[:, here(slot - HALF)], bias, slot)
+            weight = weight_of(rows, summed[:, here(slot)], bias, slot)
             within_other[:, here(slot - HALF)] = mixed(weight, q[:, at], k[:, at], v[:, at])
     part[0] = squares
     part[1] = products
@@ -259,15 +261,15 @@
 
 
 def k_mid(
-    core_ref, rows, q, k, gate, att_mine, att_other, dnormed, inward,
-    weights, turned, mixings, factor, scaled,
+    core_ref, rows, summed, q, k, gate, att_mine, att_other, dnormed,
+    weights, turned, mixings, factor, scaled, outward,
 ):
     core = core_ref[0]
     latest = latest_of(rows)
-    columns = spread(rows[0:8, :], 3)
+    outward[...] = spread(outward_of(rows, slice(0, 8)), 2)
     biased = biases(rows)
     for slot in range(8):
-        weights[slot] = weight_of(rows, columns[:, here(slot)], biased, slot)
+        weights[slot] = weight_of(rows, summed[:, here(slot)], biased, slot)
     s = lax.broadcasted_iota(jnp.int32, (TOK, HEAD_DIM), 0)
     t = lax.broadcasted_iota(jnp.int32, (TOK, HEAD_DIM), 1)
     for part in range(2):
@@ -275,12 +277,13 @@
         kept = jnp.logical_and(s <= t + part * HEAD_DIM, s.astype(F32) >= latest[:, at])
         bias = jnp.where(kept, 0.0, NEG)
         for slot in range(8):
-            turned[slot, :, at] = jnp.exp(rows[slot : slot + 1, at] - columns[:, here(slot)] + bias)
+            turned[slot, :, at] = jnp.exp(rows[slot : slot + 1, at] - summed[:, here(slot)] + bias)
+    lines = inward_of(rows)
     for slot in reversed(range(8)):
         at = cols(core, slot)
         i = slot % HALF
         query = q[:, at]
-        scaled[slot] = (query.astype(F32) * inward[:, here(slot)]).astype(BF16).T
+        scaled[slot] = turn(query, lines[slot : slot + 1, :])
         mixings[slot] = (turned[slot] * dot(k[:, at], query, 1, 1)).astype(BF16)
         att = (att_mine if slot < HALF else att_other)[:, here(i)]
         opening = jax.nn.sigmoid(gate[:, at].astype(F32))
@@ -359,20 +362,29 @@
     return (part_k + to_key * scale).astype(BF16), (part_v + to_value * scale).astype(BF16)
 
 
+def upper_dot(mixed_to, slot, right):
+    half = TOK // 2
+    return jnp.concatenate(
+        [
+            dot(mixed_to[slot, :half, :], right, 1, 0),
+            dot(mixed_to[slot, half:, half:], right[half:], 1, 0),
+        ],
+        axis=0,
+    )
+
+
 def k_end_mine(
-    core_ref, rows, q, k, v, grad_mine, grad_other, mixed_back, mixings, l_mine, gq, gate_in,
-    part_k, part_v, outward_other, k_mine, v_mine, out_q, out_gate, sems,
+    core_ref, outward, q, k, v, grad_mine, grad_other, mixed_back, mixings, l_mine, gq, gate_in,
+    part_k, part_v, k_mine, v_mine, out_q, out_gate, sems,
 ):
     core = core_ref[0]
     copies = fetch([(gq, out_q), (gate_in, out_gate)], sems)
-    outward = spread(outward_of(rows, slice(0, 8)), 2)
-    outward_other[...] = outward[:, 512:]
     for slot in range(8):
         i = slot % HALF
         at = cols(core, slot)
         upstream = (grad_mine if slot < HALF else grad_other)[:, here(i)]
-        to_key = dot(mixed_back[slot], q[:, at], 1, 0)
-        to_value = dot(mixings[slot], upstream, 1, 0)
+        to_key = upper_dot(mixed_back, slot, q[:, at])
+        to_value = upper_dot(mixings, slot, upstream)
         if slot < HALF:
             state = l_mine[i * 128 : (i + 1) * 128, :]
             k_mine[:, here(i)], v_mine[:, here(i)] = finish(
@@ -397,7 +409,7 @@
         at = cols(core, slot)
         state = l_other[i * 128 : (i + 1) * 128, :]
         kbuf[:, here(i)], vbuf[:, here(i)] = finish(
-            state, outward[:, here(i)], k[:, at], v[:, at], part_k[:, here(i)], part_v[:, here(i)]
+            state, outward[:, here(slot)], k[:, at], v[:, at], part_k[:, here(i)], part_v[:, here(i)]
         )
         for n, (buf, out) in enumerate(((kbuf, out_k), (vbuf, out_v))):
             copies.append(pltpu.make_async_copy(buf.at[:, here(i)], out.at[:, at], sems.at[2 + 2 * i + n]))
@@ -435,9 +447,9 @@
         ],
     )
     s_other = lax.ppermute(send, "seq", swap)
-    s_mine, within = call(
+    s_mine, within, summed, inward = call(
         k_local,
-        [(state_g, F32), (half, F32)],
+        [(state_g, F32), (half, F32), (wide, F32), (wide, F32)],
         0, rows, *own,
     )
     (pieces,) = call(k_pack, [((544, HEAD_DIM), F32)], 1, core, s_mine, s_other)
@@ -446,10 +458,10 @@
     entering = trade(entering).reshape(state)
     e_mine, e_send = call(k_enter, [(state, F32)] * 2, 1, core, entering, s_mine, s_other)
     e_other = lax.ppermute(e_send, "seq", swap)
-    att_mine, dnormed, within_other, part, inward = call(
+    att_mine, dnormed, within_other, part = call(
         k_attend,
-        [(half, F32), (wide, F32), (half, F32), ((2, TOK, HEAD_DIM), F32), (wide, F32)],
-        1, core, rows, q, k, v, within, e_mine, gate, gain, up,
+        [(half, F32), (wide, F32), (half, F32), ((2, TOK, HEAD_DIM), F32)],
+        1, core, rows, summed, q, k, v, within, inward, e_mine, gate, gain, up,
     )
     att_other, sums = call(
         k_sums,
@@ -457,10 +469,10 @@
         1, core, q, within_other, inward, e_other, part, dnormed,
     )
     others = [around(sums, step) for step in (2, 1, 3)]
-    weights, turned, mixings, factor, scaled = call(
+    weights, turned, mixings, factor, scaled, outward = call(
         k_mid,
-        [(square, F32), (square, F32), (square, BF16), (wide, F32), ((8, HEAD_DIM, TOK), BF16)],
-        1, core, rows, q, k, gate, att_mine, att_other, dnormed, inward,
+        [(square, F32), (square, F32), (square, BF16), (wide, F32), ((8, HEAD_DIM, TOK), BF16), (wide, F32)],
+        1, core, rows, summed, q, k, gate, att_mine, att_other, dnormed,
         cost_estimate=pl.CostEstimate(flops=4_000_000_000, bytes_accessed=8_000_000, transcendentals=1_000_000),
     )
     grad_other, b_send, inverses, projections = call(
@@ -481,11 +493,11 @@
     leaving = trade(leaving).reshape(state)
     l_mine, l_send = call(k_leave, [(state, F32)] * 2, 1, core, leaving, b_mine, b_other, s_mine, s_other)
     l_other = lax.ppermute(l_send, "seq", swap)
-    part_k, part_v, outward, k_mine, v_mine, grad_query, grad_gate = call(
+    part_k, part_v, k_mine, v_mine, grad_query, grad_gate = call(
         k_end_mine,
-        [(half, F32), (half, F32), (half, F32), (half, BF16), (half, BF16), (wide, BF16), (wide, BF16)],
-        1, core, rows, q, k, v, grad_mine, grad_other, mixed_back, mixings, l_mine, gq, grad_gate,
-        hbm_out=(5, 6),
+        [(half, F32), (half, F32), (half, BF16), (half, BF16), (wide, BF16), (wide, BF16)],
+        1, core, outward, q, k, v, grad_mine, grad_other, mixed_back, mixings, l_mine, gq, grad_gate,
+        hbm_out=(4, 5),
         scratch=[pltpu.SemaphoreType.DMA((2,))],
     )
     grad_key, grad_value = call(

time: 96.2 us -> 95.8 us (level)
  no operation moved by 1% of the time
where the time goes in v4:
time: 95.8 us; the launch traced here: 95.5 us
  blocking collectives  65.6 us (68%)
  starting transfers between devices  16.9 us (18%)
  Pallas kernels  11.4 us (12%)
    all_to_all x4, blocking collectives, trade(): return lax.all_to_all(a, 'seq', 0, 0, axis_index_groups=groups)  65.6 us
    pallas_call x15, Pallas kernels, call(): pl.pallas_call(kernel, out_shape=[jax.ShapeDtypeStruct(s, d) for s, d in...  11.4 us
    ppermute x3, starting transfers between devices, around(): lax.ppermute(a, 'head', [(i, (i + step) % heads) for i in range(heads)])  4.39 us
    ppermute x1, starting transfers between devices, local(): l_other = lax.ppermute(l_send, 'seq', swap)  3.7 us
    ppermute x1, starting transfers between devices, local(): e_other = lax.ppermute(e_send, 'seq', swap)  3.69 us
    ppermute x1, starting transfers between devices, local(): s_other = lax.ppermute(send, 'seq', swap)  3.33 us
  transfers between devices with their start and end apart: 7, of which 3 were waited for; matrix products, arithmetic and copies ran while one was open for 0% of the time, Pallas kernels for 8%

profile of v4, /device:TPU:1, one launch (start us, length us, event | category | flops | bytes accessed | tf_op | source)
XLA Modules:
  0.0 95.5 jit_solution(10721563138318826151)
XLA Ops:
  0.6 1.4 %shard_map.111 = (f32[520,128]{1,0:T(8,128)S(1)}, f32[16,256]{1,0:T(8,128)S(1)}, bf16[256,512]{1,0:T(8,128)(2,1)S(1)}, bf16[256,512]{1,0:T(8,128)(2,1)S(1)}, bf16[256,512]{1,0:T(8,128)(2,1)S(1)}) custom-call(s32[1]{0:T(128)} %bitcast.core_ref, s32[1,4]{1,0:T(1,128)} %starts_in.1, f32[8,256]{1,0:T(8,128)} %decay.1, bf16[256,1024]{1,0:T(8,128)(2,1)} %q.9, ...), custom_call_target="tpu_custom_call" | custom-call | tf_op jit(solution)/shard_map/pallas_call | solution.py:40
  2.0 0.0 copy-start
  2.1 0.0 copy-start.1
  2.1 0.0 copy-start.2
  2.1 0.0 copy-start.3
  2.1 0.0 copy-start.4
  2.1 0.0 copy-start.5
  2.1 3.3 %collective-permute-start = (f32[520,128]{1,0:T(8,128)S(1)}, f32[520,128]{1,0:T(8,128)S(1)}, u32[]{:S(2)}, u32[]{:S(2)}) collective-permute-start(f32[520,128]{1,0:T(8,128)S(1)} %get-tuple-element.54), channel_id=1, source_target_pairs={{0,4},{4,0},{8,12},{12,8},{16,20},{20,16},{24,28},{28,24},{32,36},... | collective-permute-start | bytes 798728 | tf_op jit(solution)/shard_map/ppermute | solution.py:449
  5.4 1.0 %shard_map.112 = (f32[520,128]{1,0:T(8,128)S(1)}, f32[256,512]{1,0:T(8,128)S(1)}, f32[256,1024]{1,0:T(8,128)S(1)}, f32[256,1024]{1,0:T(8,128)S(1)}) custom-call(f32[16,256]{1,0:T(8,128)S(1)} %get-tuple-element.46.rows, bf16[256,512]{1,0:T(8,128)(2,1)S(1)} %get-tuple-element.47.q, bf16[256,512]{1,0:T(8,128)(2,1)S(1)} %get-tuple-element.48.k, ...), custom_call_target="tpu_custom_call" | custom-call | tf_op jit(solution)/shard_map/pallas_call | solution.py:40
  6.5 0.1 collective-permute-done.other.s_other
  6.6 0.1 shard_map.113
  6.7 18.8 %all_to_all.20 = f32[32,1,2176]{2,1,0:T(1,128)S(1)} all-to-all(f32[32,1,2176]{2,1,0:T(1,128)S(1)} %bitcast.8), channel_id=1, replica_groups={{0,8,16,24,32,40,48,56,64,72,80,88,96,104,112,120,128,136,144,152,160,1..., dimensions={0} | all-to-all | bytes 557056 | tf_op jit(solution)/shard_map/all_to_all | solution.py:435
  25.5 0.1 shard_map.114
  25.6 16.6 %all_to_all.21 = f32[32,16,128]{2,1,0:T(8,128)S(1)} all-to-all(f32[32,16,128]{2,1,0:T(8,128)S(1)} %shard_map.114), channel_id=1, replica_groups={{0,8,16,24,32,40,48,56,64,72,80,88,96,104,112,120,128,136,144,152,160,1..., dimensions={0} | all-to-all | bytes 524288 | tf_op jit(solution)/shard_map/all_to_all | solution.py:435
  42.2 0.1 shard_map.115
  42.3 3.7 %collective-permute-start.1 = (f32[512,128]{1,0:T(8,128)S(1)}, f32[512,128]{1,0:T(8,128)S(1)}, u32[]{:S(2)}, u32[]{:S(2)}) collective-permute-start(f32[512,128]{1,0:T(8,128)S(1)} %get-tuple-element.58), channel_id=1, source_target_pairs={{0,4},{4,0},{8,12},{12,8},{16,20},{20,16},{24,28},{28,24},{32,36},... | collective-permute-start | bytes 786440 | tf_op jit(solution)/shard_map/ppermute | solution.py:460
  46.0 0.0 copy-done
  46.0 0.0 copy-done.1
  46.0 0.0 copy-done.2
  46.0 0.0 copy-done.3
  46.0 0.0 copy-done.4
  46.0 0.0 copy-done.5
  46.0 1.2 %shard_map.116 = (f32[256,512]{1,0:T(8,128)S(1)}, f32[256,1024]{1,0:T(8,128)S(1)}, f32[256,512]{1,0:T(8,128)S(1)}, f32[2,256,128]{2,1,0:T(8,128)S(1)}) custom-call(s32[1]{0:T(128)} %bitcast.core_ref, f32[16,256]{1,0:T(8,128)S(1)} %get-tuple-element.46.rows, f32[256,1024]{1,0:T(8,128)S(1)} %get-tuple-element.50.summed, bf16[256,1024]{1,0:T(8,128)(2,1)S(1)} %copy-done.2, ...), custom_call_target="tpu_custom_call" | custom-call | tf_op jit(solution)/shard_map/pallas_call | solution.py:40
  47.2 0.0 collective-permute-done.1.e_other
  47.2 0.4 shard_map.117
  47.7 2.7 %collective-permute-start.4 = (f32[8,256]{1,0:T(8,128)S(1)}, f32[8,256]{1,0:T(8,128)S(1)}, u32[]{:S(2)}, u32[]{:S(2)}) collective-permute-start(f32[8,256]{1,0:T(8,128)S(1)} %get-tuple-element.63.sums0), channel_id=1, source_target_pairs={{0,3},{1,0},{2,1},{3,2},{4,7},{5,4},{6,5},{7,6},{8,11},{9,8},{10,9... | collective-permute-start | bytes 24584 | tf_op jit(solution)/shard_map/ppermute | solution.py:438
  50.4 0.0 collective-permute-start.3
  50.4 1.6 %collective-permute-start.2 = (f32[8,256]{1,0:T(8,128)S(1)}, f32[8,256]{1,0:T(8,128)S(1)}, u32[]{:S(2)}, u32[]{:S(2)}) collective-permute-start(f32[8,256]{1,0:T(8,128)S(1)} %get-tuple-element.63.sums0), channel_id=1, source_target_pairs={{0,2},{1,3},{2,0},{3,1},{4,6},{5,7},{6,4},{7,5},{8,10},{9,11},{10,... | collective-permute-start | bytes 24584 | tf_op jit(solution)/shard_map/ppermute | solution.py:438
  52.1 1.8 %shard_map.118 = (f32[8,256,256]{2,1,0:T(8,128)S(1)}, f32[8,256,256]{2,1,0:T(8,128)S(1)}, bf16[8,256,256]{2,1,0:T(8,128)(2,1)S(1)}, f32[256,1024]{1,0:T(8,128)S(...) custom-call(s32[1]{0:T(128)} %bitcast.core_ref, f32[16,256]{1,0:T(8,128)S(1)} %get-tuple-element.46.rows, ...), custom_call_target="tpu_custom_call" | custom-call | flops 4000000000 | bytes 8000000 | tf_op jit(solution)/shard_map/pallas_call | solution.py:40
  53.9 0.0 collective-permute-done.4.sums3
  53.9 0.3 collective-permute-done.3.sums2
  54.1 0.3 collective-permute-done.2.sums1
  54.4 0.5 shard_map.119
  54.9 1.8 %collective-permute-start.5 = (f32[512,128]{1,0:T(8,128)S(1)}, f32[512,128]{1,0:T(8,128)S(1)}, u32[]{:S(2)}, u32[]{:S(2)}) collective-permute-start(f32[512,128]{1,0:T(8,128)S(1)} %get-tuple-element.75), channel_id=1, source_target_pairs={{0,4},{4,0},{8,12},{12,8},{16,20},{20,16},{24,28},{28,24},{32,36},... | collective-permute-start | bytes 786440 | tf_op jit(solution)/shard_map/ppermute | solution.py:483
  56.7 1.7 %shard_map.120 = (f32[512,128]{1,0:T(8,128)S(1)}, bf16[256,512]{1,0:T(8,128)(2,1)S(1)}, bf16[256,1024]{1,0:T(8,128)(2,1)S(1)}, bf16[256,1024]{1,0:T(8,128)(2,1)S(1)}, bf16[8,256,256]{2,1,0:T(8,128)(2,1)S(1)}) custom-call(s32[1]{0:T(128)} %bitcast.core_ref, f32[256,128]{1,0:T(8,128)S(1)} %get-tuple-element.65.inverses, ...), custom_call_target="tpu_custom_call" | custom-call | tf_op jit(solution)/shard_map/pallas_call | solution.py:40
  58.5 0.0 collective-permute-done.5.other
  58.5 0.1 shard_map.121
  58.6 14.4 %all_to_all.22.pieces = f32[32,16,128]{2,1,0:T(8,128)S(1)} all-to-all(f32[32,16,128]{2,1,0:T(8,128)S(1)} %shard_map.121), channel_id=1, replica_groups={{0,8,16,24,32,40,48,56,64,72,80,88,96,104,112,120,128,136,144,152,160,1..., dimensions={0} | all-to-all | bytes 524288 | tf_op jit(solution)/shard_map/all_to_all | solution.py:435
  72.9 0.1 shard_map.122
  73.0 15.8 %all_to_all.23 = f32[32,16,128]{2,1,0:T(8,128)S(1)} all-to-all(f32[32,16,128]{2,1,0:T(8,128)S(1)} %shard_map.122), channel_id=1, replica_groups={{0,8,16,24,32,40,48,56,64,72,80,88,96,104,112,120,128,136,144,152,160,1..., dimensions={0} | all-to-all | bytes 524288 | tf_op jit(solution)/shard_map/all_to_all | solution.py:435
  88.8 0.1 shard_map.123
  88.9 3.7 %collective-permute-start.6 = (f32[512,128]{1,0:T(8,128)S(1)}, f32[512,128]{1,0:T(8,128)S(1)}, u32[]{:S(2)}, u32[]{:S(2)}) collective-permute-start(f32[512,128]{1,0:T(8,128)S(1)} %get-tuple-element.82), channel_id=1, source_target_pairs={{0,4},{4,0},{8,12},{12,8},{16,20},{20,16},{24,28},{28,24},{32,36},... | collective-permute-start | bytes 786440 | tf_op jit(solution)/shard_map/ppermute | solution.py:495
  92.6 1.7 %shard_map.124 = (f32[256,512]{1,0:T(8,128)S(1)}, f32[256,512]{1,0:T(8,128)S(1)}, bf16[256,512]{1,0:T(8,128)(2,1)S(1)}, bf16[256,512]{1,0:T(8,128)(2,1)S(1)}, bf...) custom-call(s32[1]{0:T(128)} %bitcast.core_ref, f32[256,1024]{1,0:T(8,128)S(1)} %get-tuple-element.62.outward, ...), custom_call_target="tpu_custom_call" | custom-call | tf_op jit(solution)/shard_map/pallas_call | solution.py:40
  94.3 0.0 collective-permute-done.6.l_other
  94.3 1.2 %shard_map.125 = (bf16[256,1024]{1,0:T(8,128)(2,1)}, bf16[256,1024]{1,0:T(8,128)(2,1)}) custom-call(s32[1]{0:T(128)} %bitcast.core_ref, f32[256,1024]{1,0:T(8,128)S(1)} %get-tuple-element.62.outward, bf16[256,1024]{1,0:T(8,128)(2,1)S(1)} %copy-done, bf16[256,1024]{1,0:T(8,128)(2,1)S(1)} %copy-done.1, f32[256,512]{1,0:T(8,128)S(1)} %get-tuple-element.80.part_k, ...), custom_call_target="tpu_custom_call" | custom-call | tf_op jit(solution)/shard_map/pallas_call | solution.py:40
Async XLA Ops:
  2.0 43.9 %copy-start = (bf16[256,1024]{1,0:T(8,128)(2,1)S(1)}, bf16[256,1024]{1,0:T(8,128)(2,1)}, u32[]{:S(2)}) copy-start(bf16[256,1024]{1,0:T(8,128)(2,1)} %k.11) | copy-start | bytes 1572868
  2.1 43.9 %copy-start.1 = (bf16[256,1024]{1,0:T(8,128)(2,1)S(1)}, bf16[256,1024]{1,0:T(8,128)(2,1)}, u32[]{:S(2)}) copy-start(bf16[256,1024]{1,0:T(8,128)(2,1)} %v.9) | copy-start | bytes 1572868
  2.1 43.9 %copy-start.2 = (bf16[256,1024]{1,0:T(8,128)(2,1)S(1)}, bf16[256,1024]{1,0:T(8,128)(2,1)}, u32[]{:S(2)}) copy-start(bf16[256,1024]{1,0:T(8,128)(2,1)} %q.9) | copy-start | bytes 1572868
  2.1 43.9 %copy-start.3 = (bf16[256,1024]{1,0:T(8,128)(2,1)S(1)}, bf16[256,1024]{1,0:T(8,128)(2,1)}, u32[]{:S(2)}) copy-start(bf16[256,1024]{1,0:T(8,128)(2,1)} %up.1) | copy-start | bytes 1572868
  2.1 43.9 %copy-start.4 = (bf16[256,1024]{1,0:T(8,128)(2,1)S(1)}, bf16[256,1024]{1,0:T(8,128)(2,1)}, u32[]{:S(2)}) copy-start(bf16[256,1024]{1,0:T(8,128)(2,1)} %gate.3) | copy-start | bytes 1572868
  2.1 43.9 %copy-start.5 = (f32[1024]{0:T(1024)S(1)}, f32[1024]{0:T(1024)}, u32[]{:S(2)}) copy-start(f32[1024]{0:T(1024)} %param.14) | copy-start | bytes 12292
  2.1 4.5 %collective-permute-start = (f32[520,128]{1,0:T(8,128)S(1)}, f32[520,128]{1,0:T(8,128)S(1)}, u32[]{:S(2)}, u32[]{:S(2)}) collective-permute-start(f32[520,128]{1,0:T(8,128)S(1)} %get-tuple-element.54), channel_id=1, source_target_pairs={{0,4},{4,0},{8,12},{12,8},{16,20},{20,16},{24,28},{28,24},{32,36},... | collective-permute-start | bytes 798728 | tf_op jit(solution)/shard_map/ppermute | solution.py:449
  42.3 5.0 %collective-permute-start.1 = (f32[512,128]{1,0:T(8,128)S(1)}, f32[512,128]{1,0:T(8,128)S(1)}, u32[]{:S(2)}, u32[]{:S(2)}) collective-permute-start(f32[512,128]{1,0:T(8,128)S(1)} %get-tuple-element.58), channel_id=1, source_target_pairs={{0,4},{4,0},{8,12},{12,8},{16,20},{20,16},{24,28},{28,24},{32,36},... | collective-permute-start | bytes 786440 | tf_op jit(solution)/shard_map/ppermute | solution.py:460
  47.7 6.2 %collective-permute-start.4 = (f32[8,256]{1,0:T(8,128)S(1)}, f32[8,256]{1,0:T(8,128)S(1)}, u32[]{:S(2)}, u32[]{:S(2)}) collective-permute-start(f32[8,256]{1,0:T(8,128)S(1)} %get-tuple-element.63.sums0), channel_id=1, source_target_pairs={{0,3},{1,0},{2,1},{3,2},{4,7},{5,4},{6,5},{7,6},{8,11},{9,8},{10,9... | collective-permute-start | bytes 24584 | tf_op jit(solution)/shard_map/ppermute | solution.py:438
  50.4 3.7 %collective-permute-start.3 = (f32[8,256]{1,0:T(8,128)S(1)}, f32[8,256]{1,0:T(8,128)S(1)}, u32[]{:S(2)}, u32[]{:S(2)}) collective-permute-start(f32[8,256]{1,0:T(8,128)S(1)} %get-tuple-element.63.sums0), channel_id=1, source_target_pairs={{0,1},{1,2},{2,3},{3,0},{4,5},{5,6},{6,7},{7,4},{8,9},{9,10},{10,1... | collective-permute-start | bytes 24584 | tf_op jit(solution)/shard_map/ppermute | solution.py:438
  50.4 4.0 %collective-permute-start.2 = (f32[8,256]{1,0:T(8,128)S(1)}, f32[8,256]{1,0:T(8,128)S(1)}, u32[]{:S(2)}, u32[]{:S(2)}) collective-permute-start(f32[8,256]{1,0:T(8,128)S(1)} %get-tuple-element.63.sums0), channel_id=1, source_target_pairs={{0,2},{1,3},{2,0},{3,1},{4,6},{5,7},{6,4},{7,5},{8,10},{9,11},{10,... | collective-permute-start | bytes 24584 | tf_op jit(solution)/shard_map/ppermute | solution.py:438
  54.9 3.5 %collective-permute-start.5 = (f32[512,128]{1,0:T(8,128)S(1)}, f32[512,128]{1,0:T(8,128)S(1)}, u32[]{:S(2)}, u32[]{:S(2)}) collective-permute-start(f32[512,128]{1,0:T(8,128)S(1)} %get-tuple-element.75), channel_id=1, source_target_pairs={{0,4},{4,0},{8,12},{12,8},{16,20},{20,16},{24,28},{28,24},{32,36},... | collective-permute-start | bytes 786440 | tf_op jit(solution)/shard_map/ppermute | solution.py:483
  88.9 5.4 %collective-permute-start.6 = (f32[512,128]{1,0:T(8,128)S(1)}, f32[512,128]{1,0:T(8,128)S(1)}, u32[]{:S(2)}, u32[]{:S(2)}) collective-permute-start(f32[512,128]{1,0:T(8,128)S(1)} %get-tuple-element.82), channel_id=1, source_target_pairs={{0,4},{4,0},{8,12},{12,8},{16,20},{20,16},{24,28},{28,24},{32,36},... | collective-permute-start | bytes 786440 | tf_op jit(solution)/shard_map/ppermute | solution.py:495

commit v5 on v4

--- a/solution.py
+++ b/solution.py
@@ -308,10 +308,16 @@
     projections[...] = projection
 
 
+def query_of(grad_mixing, key, upstream, states, inward, slot):
+    i = slot % HALF
+    carried = wide_dot(upstream, states[i * 128 : (i + 1) * 128, :], 1)
+    return (dot(grad_mixing, key, 1, 0) + carried * inward[:, here(slot)]).astype(BF16)
+
+
 def k_back(
     core_ref, inverses, projections, att_mine, dnormed, grad_other, k, v,
-    weights, turned, factor, inward, scaled, e_mine, e_other,
-    mine, grad_mine, gq, gate_out, mixed_back,
+    weights, turned, factor, inward, scaled, e_mine,
+    mine, grad_mine, gq, gate_out, mixed_back, held,
 ):
     core = core_ref[0]
     inverse, projection = inverses[...], projections[...]
@@ -327,9 +333,10 @@
             upstream = grad_other[:, here(i)]
         grad_mixing = (weights[slot] * dot(upstream, value, 1, 1)).astype(BF16)
         mixed_back[slot] = (turned[slot] * dot(value, upstream, 1, 1)).astype(BF16)
-        state = (e_mine if slot < HALF else e_other)[i * 128 : (i + 1) * 128, :]
-        carried = wide_dot(upstream, state, 1)
-        gq[:, at] = (dot(grad_mixing, key, 1, 0) + carried * inward[:, here(slot)]).astype(BF16)
+        if slot < HALF:
+            gq[:, here(i)] = query_of(grad_mixing, key, upstream, e_mine, inward, slot)
+        else:
+            held[i] = grad_mixing
         gate_out[:, at] = (factor[:, here(slot)] * inverse).astype(BF16)
 
 
@@ -374,11 +381,10 @@
 
 
 def k_end_mine(
-    core_ref, outward, q, k, v, grad_mine, grad_other, mixed_back, mixings, l_mine, gq, gate_in,
-    part_k, part_v, k_mine, v_mine, out_q, out_gate, sems,
+    core_ref, outward, q, k, v, grad_mine, grad_other, mixed_back, mixings, l_mine, held, inward, e_other,
+    part_k, part_v, k_mine, v_mine, q_other,
 ):
     core = core_ref[0]
-    copies = fetch([(gq, out_q), (gate_in, out_gate)], sems)
     for slot in range(8):
         i = slot % HALF
         at = cols(core, slot)
@@ -393,17 +399,19 @@
         else:
             part_k[:, here(i)] = to_key
             part_v[:, here(i)] = to_value
-    for copy in copies:
-        copy.wait()
+            q_other[:, here(i)] = query_of(held[i], k[:, at], upstream, e_other, inward, slot)
 
 
 def k_end(
-    core_ref, outward, k, v, part_k, part_v, l_other, k_mine, v_mine,
-    out_k, out_v, kbuf, vbuf, sems,
+    core_ref, outward, k, v, part_k, part_v, l_other, k_mine, v_mine, q_mine, q_other, gate_in,
+    out_k, out_v, out_q, out_gate, kbuf, vbuf, sems,
 ):
     core = core_ref[0]
     there = half_cols(core)
-    copies = fetch([(k_mine, out_k.at[:, there]), (v_mine, out_v.at[:, there])], sems)
+    copies = fetch(
+        [(k_mine, out_k.at[:, there]), (v_mine, out_v.at[:, there]), (q_mine, out_q.at[:, there]), (q_other, out_q.at[:, half_cols(1 - core)]), (gate_in, out_gate)],
+        sems,
+    )
     for i in range(HALF):
         slot = HALF + i
         at = cols(core, slot)
@@ -412,7 +420,7 @@
             state, outward[:, here(slot)], k[:, at], v[:, at], part_k[:, here(i)], part_v[:, here(i)]
         )
         for n, (buf, out) in enumerate(((kbuf, out_k), (vbuf, out_v))):
-            copies.append(pltpu.make_async_copy(buf.at[:, here(i)], out.at[:, at], sems.at[2 + 2 * i + n]))
+            copies.append(pltpu.make_async_copy(buf.at[:, here(i)], out.at[:, at], sems.at[5 + 2 * i + n]))
             copies[-1].start()
     for copy in copies:
         copy.wait()
@@ -481,11 +489,11 @@
         0, sums, *others, att_other, dnormed, scaled,
     )
     b_other = lax.ppermute(b_send, "seq", swap)
-    b_mine, grad_mine, gq, grad_gate, mixed_back = call(
+    b_mine, grad_mine, gq, grad_gate, mixed_back, held = call(
         k_back,
-        [(state, F32), (half, BF16), (wide, BF16), (wide, BF16), (square, BF16)],
+        [(state, F32), (half, BF16), (half, BF16), (wide, BF16), (square, BF16), ((HALF, TOK, TOK), BF16)],
         1, core, inverses, projections, att_mine, dnormed, grad_other, k, v,
-        weights, turned, factor, inward, scaled, e_mine, e_other,
+        weights, turned, factor, inward, scaled, e_mine,
     )
     (back,) = call(k_pack_back, [((32, 16, HEAD_DIM), F32)], 1, core, b_mine, b_other, s_mine, s_other)
     back = trade(back)
@@ -493,19 +501,18 @@
     leaving = trade(leaving).reshape(state)
     l_mine, l_send = call(k_leave, [(state, F32)] * 2, 1, core, leaving, b_mine, b_other, s_mine, s_other)
     l_other = lax.ppermute(l_send, "seq", swap)
-    part_k, part_v, k_mine, v_mine, grad_query, grad_gate = call(
+    part_k, part_v, k_mine, v_mine, q_other = call(
         k_end_mine,
-        [(half, F32), (half, F32), (half, BF16), (half, BF16), (wide, BF16), (wide, BF16)],
-        1, core, outward, q, k, v, grad_mine, grad_other, mixed_back, mixings, l_mine, gq, grad_gate,
-        hbm_out=(4, 5),
-        scratch=[pltpu.SemaphoreType.DMA((2,))],
-    )
-    grad_key, grad_value = call(
+        [(half, F32), (half, F32), (half, BF16), (half, BF16), (half, BF16)],
+        1, core, outward, q, k, v, grad_mine, grad_other, mixed_back, mixings, l_mine,
+        held, inward, e_other,
+    )
+    grad_key, grad_value, grad_query, grad_gate = call(
         k_end,
-        [(wide, BF16), (wide, BF16)],
-        1, core, outward, k, v, part_k, part_v, l_other, k_mine, v_mine,
-        hbm_out=(0, 1),
-        scratch=[buffer, buffer, pltpu.SemaphoreType.DMA((10,))],
+        [(wide, BF16)] * 4,
+        1, core, outward, k, v, part_k, part_v, l_other, k_mine, v_mine, gq, q_other, grad_gate,
+        hbm_out=(0, 1, 2, 3),
+        scratch=[buffer, buffer, pltpu.SemaphoreType.DMA((13,))],
     )
     return grad_query, grad_key, grad_value, grad_gate
 

time: 95.8 us -> 95.3 us (level)
  transfers between devices with their start and end apart: 7 -> 7, of which waited for: 3 -> 3; matrix products, arithmetic and copies ran while one was open for 0% -> 0% of each run, Pallas kernels for 8% -> 7%
where the time goes in v5:
time: 95.3 us; the launch traced here: 95 us
  blocking collectives  65.7 us (69%)
  starting transfers between devices  16.9 us (18%)
  Pallas kernels  10.8 us (11%)
    all_to_all x4, blocking collectives, trade(): return lax.all_to_all(a, 'seq', 0, 0, axis_index_groups=groups)  65.7 us
    pallas_call x15, Pallas kernels, call(): pl.pallas_call(kernel, out_shape=[jax.ShapeDtypeStruct(s, d) for s, d in...  10.8 us
    ppermute x3, starting transfers between devices, around(): lax.ppermute(a, 'head', [(i, (i + step) % heads) for i in range(heads)])  4.39 us
    ppermute x1, starting transfers between devices, local(): l_other = lax.ppermute(l_send, 'seq', swap)  3.7 us
    ppermute x1, starting transfers between devices, local(): e_other = lax.ppermute(e_send, 'seq', swap)  3.69 us
    ppermute x1, starting transfers between devices, local(): s_other = lax.ppermute(send, 'seq', swap)  3.33 us
  transfers between devices with their start and end apart: 7, of which 3 were waited for; matrix products, arithmetic and copies ran while one was open for 0% of the time, Pallas kernels for 7%

profile of v5, /device:TPU:1, one launch (start us, length us, event | category | flops | bytes accessed | tf_op | source)
XLA Modules:
  0.0 95.0 jit_solution(5702088256029956004)
XLA Ops:
  0.6 1.4 %shard_map.111 = (f32[520,128]{1,0:T(8,128)S(1)}, f32[16,256]{1,0:T(8,128)S(1)}, bf16[256,512]{1,0:T(8,128)(2,1)S(1)}, bf16[256,512]{1,0:T(8,128)(2,1)S(1)}, bf16[256,512]{1,0:T(8,128)(2,1)S(1)}) custom-call(s32[1]{0:T(128)} %bitcast.core_ref, s32[1,4]{1,0:T(1,128)} %starts_in.1, f32[8,256]{1,0:T(8,128)} %decay.1, bf16[256,1024]{1,0:T(8,128)(2,1)} %q.9, ...), custom_call_target="tpu_custom_call" | custom-call | tf_op jit(solution)/shard_map/pallas_call | solution.py:40
  2.0 0.0 copy-start
  2.1 0.0 copy-start.1
  2.1 0.0 copy-start.2
  2.1 0.0 copy-start.3
  2.1 0.0 copy-start.4
  2.1 0.0 copy-start.5
  2.1 3.3 %collective-permute-start = (f32[520,128]{1,0:T(8,128)S(1)}, f32[520,128]{1,0:T(8,128)S(1)}, u32[]{:S(2)}, u32[]{:S(2)}) collective-permute-start(f32[520,128]{1,0:T(8,128)S(1)} %get-tuple-element.56), channel_id=1, source_target_pairs={{0,4},{4,0},{8,12},{12,8},{16,20},{20,16},{24,28},{28,24},{32,36},... | collective-permute-start | bytes 798728 | tf_op jit(solution)/shard_map/ppermute | solution.py:457
  5.4 1.0 %shard_map.112 = (f32[520,128]{1,0:T(8,128)S(1)}, f32[256,512]{1,0:T(8,128)S(1)}, f32[256,1024]{1,0:T(8,128)S(1)}, f32[256,1024]{1,0:T(8,128)S(1)}) custom-call(f32[16,256]{1,0:T(8,128)S(1)} %get-tuple-element.48.rows, bf16[256,512]{1,0:T(8,128)(2,1)S(1)} %get-tuple-element.49.q, bf16[256,512]{1,0:T(8,128)(2,1)S(1)} %get-tuple-element.50.k, ...), custom_call_target="tpu_custom_call" | custom-call | tf_op jit(solution)/shard_map/pallas_call | solution.py:40
  6.5 0.1 collective-permute-done.other.s_other
  6.6 0.1 shard_map.113
  6.7 18.8 %all_to_all.20 = f32[32,1,2176]{2,1,0:T(1,128)S(1)} all-to-all(f32[32,1,2176]{2,1,0:T(1,128)S(1)} %bitcast.8), channel_id=1, replica_groups={{0,8,16,24,32,40,48,56,64,72,80,88,96,104,112,120,128,136,144,152,160,1..., dimensions={0} | all-to-all | bytes 557056 | tf_op jit(solution)/shard_map/all_to_all | solution.py:443
  25.5 0.1 shard_map.114
  25.6 16.6 %all_to_all.21 = f32[32,16,128]{2,1,0:T(8,128)S(1)} all-to-all(f32[32,16,128]{2,1,0:T(8,128)S(1)} %shard_map.114), channel_id=1, replica_groups={{0,8,16,24,32,40,48,56,64,72,80,88,96,104,112,120,128,136,144,152,160,1..., dimensions={0} | all-to-all | bytes 524288 | tf_op jit(solution)/shard_map/all_to_all | solution.py:443
  42.2 0.1 shard_map.115
  42.3 3.7 %collective-permute-start.1 = (f32[512,128]{1,0:T(8,128)S(1)}, f32[512,128]{1,0:T(8,128)S(1)}, u32[]{:S(2)}, u32[]{:S(2)}) collective-permute-start(f32[512,128]{1,0:T(8,128)S(1)} %get-tuple-element.60), channel_id=1, source_target_pairs={{0,4},{4,0},{8,12},{12,8},{16,20},{20,16},{24,28},{28,24},{32,36},... | collective-permute-start | bytes 786440 | tf_op jit(solution)/shard_map/ppermute | solution.py:468
  46.0 0.0 copy-done
  46.0 0.0 copy-done.1
  46.0 0.0 copy-done.2
  46.0 0.0 copy-done.3
  46.0 0.0 copy-done.4
  46.0 0.0 copy-done.5
  46.0 1.2 %shard_map.116 = (f32[256,512]{1,0:T(8,128)S(1)}, f32[256,1024]{1,0:T(8,128)S(1)}, f32[256,512]{1,0:T(8,128)S(1)}, f32[2,256,128]{2,1,0:T(8,128)S(1)}) custom-call(s32[1]{0:T(128)} %bitcast.core_ref, f32[16,256]{1,0:T(8,128)S(1)} %get-tuple-element.48.rows, f32[256,1024]{1,0:T(8,128)S(1)} %get-tuple-element.52.summed, bf16[256,1024]{1,0:T(8,128)(2,1)S(1)} %copy-done.2, ...), custom_call_target="tpu_custom_call" | custom-call | tf_op jit(solution)/shard_map/pallas_call | solution.py:40
  47.2 0.0 collective-permute-done.1.e_other
  47.2 0.4 shard_map.117
  47.7 2.7 %collective-permute-start.4 = (f32[8,256]{1,0:T(8,128)S(1)}, f32[8,256]{1,0:T(8,128)S(1)}, u32[]{:S(2)}, u32[]{:S(2)}) collective-permute-start(f32[8,256]{1,0:T(8,128)S(1)} %get-tuple-element.65.sums0), channel_id=1, source_target_pairs={{0,3},{1,0},{2,1},{3,2},{4,7},{5,4},{6,5},{7,6},{8,11},{9,8},{10,9... | collective-permute-start | bytes 24584 | tf_op jit(solution)/shard_map/ppermute | solution.py:446
  50.4 0.0 collective-permute-start.3
  50.4 1.6 %collective-permute-start.2 = (f32[8,256]{1,0:T(8,128)S(1)}, f32[8,256]{1,0:T(8,128)S(1)}, u32[]{:S(2)}, u32[]{:S(2)}) collective-permute-start(f32[8,256]{1,0:T(8,128)S(1)} %get-tuple-element.65.sums0), channel_id=1, source_target_pairs={{0,2},{1,3},{2,0},{3,1},{4,6},{5,7},{6,4},{7,5},{8,10},{9,11},{10,... | collective-permute-start | bytes 24584 | tf_op jit(solution)/shard_map/ppermute | solution.py:446
  52.1 1.8 %shard_map.118 = (f32[8,256,256]{2,1,0:T(8,128)S(1)}, f32[8,256,256]{2,1,0:T(8,128)S(1)}, bf16[8,256,256]{2,1,0:T(8,128)(2,1)S(1)}, f32[256,1024]{1,0:T(8,128)S(...) custom-call(s32[1]{0:T(128)} %bitcast.core_ref, f32[16,256]{1,0:T(8,128)S(1)} %get-tuple-element.48.rows, ...), custom_call_target="tpu_custom_call" | custom-call | flops 4000000000 | bytes 8000000 | tf_op jit(solution)/shard_map/pallas_call | solution.py:40
  53.9 0.0 collective-permute-done.4.sums3
  53.9 0.3 collective-permute-done.3.sums2
  54.1 0.3 collective-permute-done.2.sums1
  54.4 0.5 shard_map.119
  54.9 1.8 %collective-permute-start.5 = (f32[512,128]{1,0:T(8,128)S(1)}, f32[512,128]{1,0:T(8,128)S(1)}, u32[]{:S(2)}, u32[]{:S(2)}) collective-permute-start(f32[512,128]{1,0:T(8,128)S(1)} %get-tuple-element.77), channel_id=1, source_target_pairs={{0,4},{4,0},{8,12},{12,8},{16,20},{20,16},{24,28},{28,24},{32,36},... | collective-permute-start | bytes 786440 | tf_op jit(solution)/shard_map/ppermute | solution.py:491
  56.7 1.4 %shard_map.120 = (f32[512,128]{1,0:T(8,128)S(1)}, bf16[256,512]{1,0:T(8,128)(2,1)S(1)}, bf16[256,512]{1,0:T(8,128)(2,1)S(1)}, bf16[256,1024]{1,0:T(8,128)(2,1)S(...) custom-call(s32[1]{0:T(128)} %bitcast.core_ref, f32[256,128]{1,0:T(8,128)S(1)} %get-tuple-element.67.inverses, ...), custom_call_target="tpu_custom_call" | custom-call | tf_op jit(solution)/shard_map/pallas_call | solution.py:40
  58.1 0.0 collective-permute-done.5.other
  58.2 0.1 shard_map.121
  58.2 14.2 %all_to_all.22.pieces = f32[32,16,128]{2,1,0:T(8,128)S(1)} all-to-all(f32[32,16,128]{2,1,0:T(8,128)S(1)} %shard_map.121), channel_id=1, replica_groups={{0,8,16,24,32,40,48,56,64,72,80,88,96,104,112,120,128,136,144,152,160,1..., dimensions={0} | all-to-all | bytes 524288 | tf_op jit(solution)/shard_map/all_to_all | solution.py:443
  72.4 0.1 shard_map.122
  72.4 16.0 %all_to_all.23 = f32[32,16,128]{2,1,0:T(8,128)S(1)} all-to-all(f32[32,16,128]{2,1,0:T(8,128)S(1)} %shard_map.122), channel_id=1, replica_groups={{0,8,16,24,32,40,48,56,64,72,80,88,96,104,112,120,128,136,144,152,160,1..., dimensions={0} | all-to-all | bytes 524288 | tf_op jit(solution)/shard_map/all_to_all | solution.py:443
  88.5 0.1 shard_map.123
  88.6 3.7 %collective-permute-start.6 = (f32[512,128]{1,0:T(8,128)S(1)}, f32[512,128]{1,0:T(8,128)S(1)}, u32[]{:S(2)}, u32[]{:S(2)}) collective-permute-start(f32[512,128]{1,0:T(8,128)S(1)} %get-tuple-element.82), channel_id=1, source_target_pairs={{0,4},{4,0},{8,12},{12,8},{16,20},{20,16},{24,28},{28,24},{32,36},... | collective-permute-start | bytes 786440 | tf_op jit(solution)/shard_map/ppermute | solution.py:503
  92.3 1.2 %shard_map.124 = (f32[256,512]{1,0:T(8,128)S(1)}, f32[256,512]{1,0:T(8,128)S(1)}, bf16[256,512]{1,0:T(8,128)(2,1)S(1)}, bf16[256,512]{1,0:T(8,128)(2,1)S(1)}, bf16[256,512]{1,0:T(8,128)(2,1)S(1)}) custom-call(s32[1]{0:T(128)} %bitcast.core_ref, f32[256,1024]{1,0:T(8,128)S(1)} %get-tuple-element.64.outward, bf16[256,1024]{1,0:T(8,128)(2,1)S(1)} %copy-done.2, ...), custom_call_target="tpu_custom_call" | custom-call | tf_op jit(solution)/shard_map/pallas_call | solution.py:40
  93.5 0.0 collective-permute-done.6.l_other
  93.5 1.5 %shard_map.125 = (bf16[256,1024]{1,0:T(8,128)(2,1)}, bf16[256,1024]{1,0:T(8,128)(2,1)}, bf16[256,1024]{1,0:T(8,128)(2,1)}, bf16[256,1024]{1,0:T(8,128)(2,1)}) custom-call(s32[1]{0:T(128)} %bitcast.core_ref, f32[256,1024]{1,0:T(8,128)S(1)} %get-tuple-element.64.outward, bf16[256,1024]{1,0:T(8,128)(2,1)S(1)} %copy-done, bf16[256,1024]{1,0:T(8,128)(2,1)S(1)} %copy-done.1, ...), custom_call_target="tpu_custom_call" | custom-call | tf_op jit(solution)/shard_map/pallas_call | solution.py:40
Async XLA Ops:
  2.0 43.9 %copy-start = (bf16[256,1024]{1,0:T(8,128)(2,1)S(1)}, bf16[256,1024]{1,0:T(8,128)(2,1)}, u32[]{:S(2)}) copy-start(bf16[256,1024]{1,0:T(8,128)(2,1)} %k.11) | copy-start | bytes 1572868
  2.1 43.9 %copy-start.1 = (bf16[256,1024]{1,0:T(8,128)(2,1)S(1)}, bf16[256,1024]{1,0:T(8,128)(2,1)}, u32[]{:S(2)}) copy-start(bf16[256,1024]{1,0:T(8,128)(2,1)} %v.9) | copy-start | bytes 1572868
  2.1 43.9 %copy-start.2 = (bf16[256,1024]{1,0:T(8,128)(2,1)S(1)}, bf16[256,1024]{1,0:T(8,128)(2,1)}, u32[]{:S(2)}) copy-start(bf16[256,1024]{1,0:T(8,128)(2,1)} %q.9) | copy-start | bytes 1572868
  2.1 43.9 %copy-start.3 = (bf16[256,1024]{1,0:T(8,128)(2,1)S(1)}, bf16[256,1024]{1,0:T(8,128)(2,1)}, u32[]{:S(2)}) copy-start(bf16[256,1024]{1,0:T(8,128)(2,1)} %up.1) | copy-start | bytes 1572868
  2.1 43.9 %copy-start.4 = (bf16[256,1024]{1,0:T(8,128)(2,1)S(1)}, bf16[256,1024]{1,0:T(8,128)(2,1)}, u32[]{:S(2)}) copy-start(bf16[256,1024]{1,0:T(8,128)(2,1)} %gate.3) | copy-start | bytes 1572868
  2.1 43.9 %copy-start.5 = (f32[1024]{0:T(1024)S(1)}, f32[1024]{0:T(1024)}, u32[]{:S(2)}) copy-start(f32[1024]{0:T(1024)} %param.14) | copy-start | bytes 12292
  2.1 4.5 %collective-permute-start = (f32[520,128]{1,0:T(8,128)S(1)}, f32[520,128]{1,0:T(8,128)S(1)}, u32[]{:S(2)}, u32[]{:S(2)}) collective-permute-start(f32[520,128]{1,0:T(8,128)S(1)} %get-tuple-element.56), channel_id=1, source_target_pairs={{0,4},{4,0},{8,12},{12,8},{16,20},{20,16},{24,28},{28,24},{32,36},... | collective-permute-start | bytes 798728 | tf_op jit(solution)/shard_map/ppermute | solution.py:457
  42.3 5.0 %collective-permute-start.1 = (f32[512,128]{1,0:T(8,128)S(1)}, f32[512,128]{1,0:T(8,128)S(1)}, u32[]{:S(2)}, u32[]{:S(2)}) collective-permute-start(f32[512,128]{1,0:T(8,128)S(1)} %get-tuple-element.60), channel_id=1, source_target_pairs={{0,4},{4,0},{8,12},{12,8},{16,20},{20,16},{24,28},{28,24},{32,36},... | collective-permute-start | bytes 786440 | tf_op jit(solution)/shard_map/ppermute | solution.py:468
  47.7 6.2 %collective-permute-start.4 = (f32[8,256]{1,0:T(8,128)S(1)}, f32[8,256]{1,0:T(8,128)S(1)}, u32[]{:S(2)}, u32[]{:S(2)}) collective-permute-start(f32[8,256]{1,0:T(8,128)S(1)} %get-tuple-element.65.sums0), channel_id=1, source_target_pairs={{0,3},{1,0},{2,1},{3,2},{4,7},{5,4},{6,5},{7,6},{8,11},{9,8},{10,9... | collective-permute-start | bytes 24584 | tf_op jit(solution)/shard_map/ppermute | solution.py:446
  50.4 3.7 %collective-permute-start.3 = (f32[8,256]{1,0:T(8,128)S(1)}, f32[8,256]{1,0:T(8,128)S(1)}, u32[]{:S(2)}, u32[]{:S(2)}) collective-permute-start(f32[8,256]{1,0:T(8,128)S(1)} %get-tuple-element.65.sums0), channel_id=1, source_target_pairs={{0,1},{1,2},{2,3},{3,0},{4,5},{5,6},{6,7},{7,4},{8,9},{9,10},{10,1... | collective-permute-start | bytes 24584 | tf_op jit(solution)/shard_map/ppermute | solution.py:446
  50.4 4.0 %collective-permute-start.2 = (f32[8,256]{1,0:T(8,128)S(1)}, f32[8,256]{1,0:T(8,128)S(1)}, u32[]{:S(2)}, u32[]{:S(2)}) collective-permute-start(f32[8,256]{1,0:T(8,128)S(1)} %get-tuple-element.65.sums0), channel_id=1, source_target_pairs={{0,2},{1,3},{2,0},{3,1},{4,6},{5,7},{6,4},{7,5},{8,10},{9,11},{10,... | collective-permute-start | bytes 24584 | tf_op jit(solution)/shard_map/ppermute | solution.py:446
  54.9 3.2 %collective-permute-start.5 = (f32[512,128]{1,0:T(8,128)S(1)}, f32[512,128]{1,0:T(8,128)S(1)}, u32[]{:S(2)}, u32[]{:S(2)}) collective-permute-start(f32[512,128]{1,0:T(8,128)S(1)} %get-tuple-element.77), channel_id=1, source_target_pairs={{0,4},{4,0},{8,12},{12,8},{16,20},{20,16},{24,28},{28,24},{32,36},... | collective-permute-start | bytes 786440 | tf_op jit(solution)/shard_map/ppermute | solution.py:491
  88.6 4.9 %collective-permute-start.6 = (f32[512,128]{1,0:T(8,128)S(1)}, f32[512,128]{1,0:T(8,128)S(1)}, u32[]{:S(2)}, u32[]{:S(2)}) collective-permute-start(f32[512,128]{1,0:T(8,128)S(1)} %get-tuple-element.82), channel_id=1, source_target_pairs={{0,4},{4,0},{8,12},{12,8},{16,20},{20,16},{24,28},{28,24},{32,36},... | collective-permute-start | bytes 786440 | tf_op jit(solution)/shard_map/ppermute | solution.py:503

commit v6 on v5

--- a/solution.py
+++ b/solution.py
@@ -419,8 +419,13 @@
         kbuf[:, here(i)], vbuf[:, here(i)] = finish(
             state, outward[:, here(slot)], k[:, at], v[:, at], part_k[:, here(i)], part_v[:, here(i)]
         )
+        if i % 2 == 0:
+            continue
+        pair = slice((i - 1) * HEAD_DIM, (i + 1) * HEAD_DIM)
+        begin = pl.multiple_of((1 - core) * 512 + (i - 1) * HEAD_DIM, 2 * HEAD_DIM)
         for n, (buf, out) in enumerate(((kbuf, out_k), (vbuf, out_v))):
-            copies.append(pltpu.make_async_copy(buf.at[:, here(i)], out.at[:, at], sems.at[5 + 2 * i + n]))
+            target = out.at[:, pl.ds(begin, 2 * HEAD_DIM)]
+            copies.append(pltpu.make_async_copy(buf.at[:, pair], target, sems.at[5 + 2 * i + n]))
             copies[-1].start()
     for copy in copies:
         copy.wait()

time: 95.3 us -> 95.4 us (level)
  no operation moved by 1% of the time
where the time goes in v6:
time: 95.4 us; the launch traced here: 95.1 us
  blocking collectives  65.7 us (69%)
  starting transfers between devices  16.9 us (18%)
  Pallas kernels  11 us (12%)
    all_to_all x4, blocking collectives, trade(): return lax.all_to_all(a, 'seq', 0, 0, axis_index_groups=groups)  65.7 us
    pallas_call x15, Pallas kernels, call(): pl.pallas_call(kernel, out_shape=[jax.ShapeDtypeStruct(s, d) for s, d in...  11 us
    ppermute x3, starting transfers between devices, around(): lax.ppermute(a, 'head', [(i, (i + step) % heads) for i in range(heads)])  4.39 us
    ppermute x1, starting transfers between devices, local(): l_other = lax.ppermute(l_send, 'seq', swap)  3.7 us
    ppermute x1, starting transfers between devices, local(): e_other = lax.ppermute(e_send, 'seq', swap)  3.69 us
    ppermute x1, starting transfers between devices, local(): s_other = lax.ppermute(send, 'seq', swap)  3.33 us
  transfers between devices with their start and end apart: 7, of which 3 were waited for; matrix products, arithmetic and copies ran while one was open for 0% of the time, Pallas kernels for 7%

profile of v6, /device:TPU:1, one launch (start us, length us, event | category | flops | bytes accessed | tf_op | source)
XLA Modules:
  0.0 95.1 jit_solution(2287902921146181764)
XLA Ops:
  0.6 1.4 %shard_map.111 = (f32[520,128]{1,0:T(8,128)S(1)}, f32[16,256]{1,0:T(8,128)S(1)}, bf16[256,512]{1,0:T(8,128)(2,1)S(1)}, bf16[256,512]{1,0:T(8,128)(2,1)S(1)}, bf16[256,512]{1,0:T(8,128)(2,1)S(1)}) custom-call(s32[1]{0:T(128)} %bitcast.core_ref, s32[1,4]{1,0:T(1,128)} %starts_in.1, f32[8,256]{1,0:T(8,128)} %decay.1, bf16[256,1024]{1,0:T(8,128)(2,1)} %q.9, ...), custom_call_target="tpu_custom_call" | custom-call | tf_op jit(solution)/shard_map/pallas_call | solution.py:40
  2.0 0.0 copy-start
  2.1 0.0 copy-start.1
  2.1 0.0 copy-start.2
  2.1 0.0 copy-start.3
  2.1 0.0 copy-start.4
  2.1 0.0 copy-start.5
  2.1 3.3 %collective-permute-start = (f32[520,128]{1,0:T(8,128)S(1)}, f32[520,128]{1,0:T(8,128)S(1)}, u32[]{:S(2)}, u32[]{:S(2)}) collective-permute-start(f32[520,128]{1,0:T(8,128)S(1)} %get-tuple-element.56), channel_id=1, source_target_pairs={{0,4},{4,0},{8,12},{12,8},{16,20},{20,16},{24,28},{28,24},{32,36},... | collective-permute-start | bytes 798728 | tf_op jit(solution)/shard_map/ppermute | solution.py:462
  5.4 1.0 %shard_map.112 = (f32[520,128]{1,0:T(8,128)S(1)}, f32[256,512]{1,0:T(8,128)S(1)}, f32[256,1024]{1,0:T(8,128)S(1)}, f32[256,1024]{1,0:T(8,128)S(1)}) custom-call(f32[16,256]{1,0:T(8,128)S(1)} %get-tuple-element.48.rows, bf16[256,512]{1,0:T(8,128)(2,1)S(1)} %get-tuple-element.49.q, bf16[256,512]{1,0:T(8,128)(2,1)S(1)} %get-tuple-element.50.k, ...), custom_call_target="tpu_custom_call" | custom-call | tf_op jit(solution)/shard_map/pallas_call | solution.py:40
  6.5 0.1 collective-permute-done.other.s_other
  6.6 0.1 shard_map.113
  6.7 18.8 %all_to_all.20 = f32[32,1,2176]{2,1,0:T(1,128)S(1)} all-to-all(f32[32,1,2176]{2,1,0:T(1,128)S(1)} %bitcast.8), channel_id=1, replica_groups={{0,8,16,24,32,40,48,56,64,72,80,88,96,104,112,120,128,136,144,152,160,1..., dimensions={0} | all-to-all | bytes 557056 | tf_op jit(solution)/shard_map/all_to_all | solution.py:448
  25.5 0.1 shard_map.114
  25.6 16.6 %all_to_all.21 = f32[32,16,128]{2,1,0:T(8,128)S(1)} all-to-all(f32[32,16,128]{2,1,0:T(8,128)S(1)} %shard_map.114), channel_id=1, replica_groups={{0,8,16,24,32,40,48,56,64,72,80,88,96,104,112,120,128,136,144,152,160,1..., dimensions={0} | all-to-all | bytes 524288 | tf_op jit(solution)/shard_map/all_to_all | solution.py:448
  42.2 0.1 shard_map.115
  42.3 3.7 %collective-permute-start.1 = (f32[512,128]{1,0:T(8,128)S(1)}, f32[512,128]{1,0:T(8,128)S(1)}, u32[]{:S(2)}, u32[]{:S(2)}) collective-permute-start(f32[512,128]{1,0:T(8,128)S(1)} %get-tuple-element.60), channel_id=1, source_target_pairs={{0,4},{4,0},{8,12},{12,8},{16,20},{20,16},{24,28},{28,24},{32,36},... | collective-permute-start | bytes 786440 | tf_op jit(solution)/shard_map/ppermute | solution.py:473
  46.0 0.0 copy-done
  46.0 0.0 copy-done.1
  46.0 0.0 copy-done.2
  46.0 0.0 copy-done.3
  46.0 0.0 copy-done.4
  46.0 0.0 copy-done.5
  46.0 1.2 %shard_map.116 = (f32[256,512]{1,0:T(8,128)S(1)}, f32[256,1024]{1,0:T(8,128)S(1)}, f32[256,512]{1,0:T(8,128)S(1)}, f32[2,256,128]{2,1,0:T(8,128)S(1)}) custom-call(s32[1]{0:T(128)} %bitcast.core_ref, f32[16,256]{1,0:T(8,128)S(1)} %get-tuple-element.48.rows, f32[256,1024]{1,0:T(8,128)S(1)} %get-tuple-element.52.summed, bf16[256,1024]{1,0:T(8,128)(2,1)S(1)} %copy-done.2, ...), custom_call_target="tpu_custom_call" | custom-call | tf_op jit(solution)/shard_map/pallas_call | solution.py:40
  47.2 0.0 collective-permute-done.1.e_other
  47.2 0.4 shard_map.117
  47.7 2.7 %collective-permute-start.4 = (f32[8,256]{1,0:T(8,128)S(1)}, f32[8,256]{1,0:T(8,128)S(1)}, u32[]{:S(2)}, u32[]{:S(2)}) collective-permute-start(f32[8,256]{1,0:T(8,128)S(1)} %get-tuple-element.65.sums0), channel_id=1, source_target_pairs={{0,3},{1,0},{2,1},{3,2},{4,7},{5,4},{6,5},{7,6},{8,11},{9,8},{10,9... | collective-permute-start | bytes 24584 | tf_op jit(solution)/shard_map/ppermute | solution.py:451
  50.4 0.0 collective-permute-start.3
  50.4 1.6 %collective-permute-start.2 = (f32[8,256]{1,0:T(8,128)S(1)}, f32[8,256]{1,0:T(8,128)S(1)}, u32[]{:S(2)}, u32[]{:S(2)}) collective-permute-start(f32[8,256]{1,0:T(8,128)S(1)} %get-tuple-element.65.sums0), channel_id=1, source_target_pairs={{0,2},{1,3},{2,0},{3,1},{4,6},{5,7},{6,4},{7,5},{8,10},{9,11},{10,... | collective-permute-start | bytes 24584 | tf_op jit(solution)/shard_map/ppermute | solution.py:451
  52.1 1.8 %shard_map.118 = (f32[8,256,256]{2,1,0:T(8,128)S(1)}, f32[8,256,256]{2,1,0:T(8,128)S(1)}, bf16[8,256,256]{2,1,0:T(8,128)(2,1)S(1)}, f32[256,1024]{1,0:T(8,128)S(...) custom-call(s32[1]{0:T(128)} %bitcast.core_ref, f32[16,256]{1,0:T(8,128)S(1)} %get-tuple-element.48.rows, ...), custom_call_target="tpu_custom_call" | custom-call | flops 4000000000 | bytes 8000000 | tf_op jit(solution)/shard_map/pallas_call | solution.py:40
  53.9 0.0 collective-permute-done.4.sums3
  53.9 0.3 collective-permute-done.3.sums2
  54.1 0.3 collective-permute-done.2.sums1
  54.4 0.5 shard_map.119
  54.9 1.8 %collective-permute-start.5 = (f32[512,128]{1,0:T(8,128)S(1)}, f32[512,128]{1,0:T(8,128)S(1)}, u32[]{:S(2)}, u32[]{:S(2)}) collective-permute-start(f32[512,128]{1,0:T(8,128)S(1)} %get-tuple-element.77), channel_id=1, source_target_pairs={{0,4},{4,0},{8,12},{12,8},{16,20},{20,16},{24,28},{28,24},{32,36},... | collective-permute-start | bytes 786440 | tf_op jit(solution)/shard_map/ppermute | solution.py:496
  56.7 1.4 %shard_map.120 = (f32[512,128]{1,0:T(8,128)S(1)}, bf16[256,512]{1,0:T(8,128)(2,1)S(1)}, bf16[256,512]{1,0:T(8,128)(2,1)S(1)}, bf16[256,1024]{1,0:T(8,128)(2,1)S(...) custom-call(s32[1]{0:T(128)} %bitcast.core_ref, f32[256,128]{1,0:T(8,128)S(1)} %get-tuple-element.67.inverses, ...), custom_call_target="tpu_custom_call" | custom-call | tf_op jit(solution)/shard_map/pallas_call | solution.py:40
  58.1 0.0 collective-permute-done.5.other
  58.2 0.1 shard_map.121
  58.2 14.2 %all_to_all.22.pieces = f32[32,16,128]{2,1,0:T(8,128)S(1)} all-to-all(f32[32,16,128]{2,1,0:T(8,128)S(1)} %shard_map.121), channel_id=1, replica_groups={{0,8,16,24,32,40,48,56,64,72,80,88,96,104,112,120,128,136,144,152,160,1..., dimensions={0} | all-to-all | bytes 524288 | tf_op jit(solution)/shard_map/all_to_all | solution.py:448
  72.4 0.1 shard_map.122
  72.4 16.0 %all_to_all.23 = f32[32,16,128]{2,1,0:T(8,128)S(1)} all-to-all(f32[32,16,128]{2,1,0:T(8,128)S(1)} %shard_map.122), channel_id=1, replica_groups={{0,8,16,24,32,40,48,56,64,72,80,88,96,104,112,120,128,136,144,152,160,1..., dimensions={0} | all-to-all | bytes 524288 | tf_op jit(solution)/shard_map/all_to_all | solution.py:448
  88.5 0.1 shard_map.123
  88.6 3.7 %collective-permute-start.6 = (f32[512,128]{1,0:T(8,128)S(1)}, f32[512,128]{1,0:T(8,128)S(1)}, u32[]{:S(2)}, u32[]{:S(2)}) collective-permute-start(f32[512,128]{1,0:T(8,128)S(1)} %get-tuple-element.82), channel_id=1, source_target_pairs={{0,4},{4,0},{8,12},{12,8},{16,20},{20,16},{24,28},{28,24},{32,36},... | collective-permute-start | bytes 786440 | tf_op jit(solution)/shard_map/ppermute | solution.py:508
  92.3 1.2 %shard_map.124 = (f32[256,512]{1,0:T(8,128)S(1)}, f32[256,512]{1,0:T(8,128)S(1)}, bf16[256,512]{1,0:T(8,128)(2,1)S(1)}, bf16[256,512]{1,0:T(8,128)(2,1)S(1)}, bf16[256,512]{1,0:T(8,128)(2,1)S(1)}) custom-call(s32[1]{0:T(128)} %bitcast.core_ref, f32[256,1024]{1,0:T(8,128)S(1)} %get-tuple-element.64.outward, bf16[256,1024]{1,0:T(8,128)(2,1)S(1)} %copy-done.2, ...), custom_call_target="tpu_custom_call" | custom-call | tf_op jit(solution)/shard_map/pallas_call | solution.py:40
  93.5 0.0 collective-permute-done.6.l_other
  93.5 1.6 %shard_map.125 = (bf16[256,1024]{1,0:T(8,128)(2,1)}, bf16[256,1024]{1,0:T(8,128)(2,1)}, bf16[256,1024]{1,0:T(8,128)(2,1)}, bf16[256,1024]{1,0:T(8,128)(2,1)}) custom-call(s32[1]{0:T(128)} %bitcast.core_ref, f32[256,1024]{1,0:T(8,128)S(1)} %get-tuple-element.64.outward, bf16[256,1024]{1,0:T(8,128)(2,1)S(1)} %copy-done, bf16[256,1024]{1,0:T(8,128)(2,1)S(1)} %copy-done.1, ...), custom_call_target="tpu_custom_call" | custom-call | tf_op jit(solution)/shard_map/pallas_call | solution.py:40
Async XLA Ops:
  2.0 43.9 %copy-start = (bf16[256,1024]{1,0:T(8,128)(2,1)S(1)}, bf16[256,1024]{1,0:T(8,128)(2,1)}, u32[]{:S(2)}) copy-start(bf16[256,1024]{1,0:T(8,128)(2,1)} %k.11) | copy-start | bytes 1572868
  2.1 43.9 %copy-start.1 = (bf16[256,1024]{1,0:T(8,128)(2,1)S(1)}, bf16[256,1024]{1,0:T(8,128)(2,1)}, u32[]{:S(2)}) copy-start(bf16[256,1024]{1,0:T(8,128)(2,1)} %v.9) | copy-start | bytes 1572868
  2.1 43.9 %copy-start.2 = (bf16[256,1024]{1,0:T(8,128)(2,1)S(1)}, bf16[256,1024]{1,0:T(8,128)(2,1)}, u32[]{:S(2)}) copy-start(bf16[256,1024]{1,0:T(8,128)(2,1)} %q.9) | copy-start | bytes 1572868
  2.1 43.9 %copy-start.3 = (bf16[256,1024]{1,0:T(8,128)(2,1)S(1)}, bf16[256,1024]{1,0:T(8,128)(2,1)}, u32[]{:S(2)}) copy-start(bf16[256,1024]{1,0:T(8,128)(2,1)} %up.1) | copy-start | bytes 1572868
  2.1 43.9 %copy-start.4 = (bf16[256,1024]{1,0:T(8,128)(2,1)S(1)}, bf16[256,1024]{1,0:T(8,128)(2,1)}, u32[]{:S(2)}) copy-start(bf16[256,1024]{1,0:T(8,128)(2,1)} %gate.3) | copy-start | bytes 1572868
  2.1 43.9 %copy-start.5 = (f32[1024]{0:T(1024)S(1)}, f32[1024]{0:T(1024)}, u32[]{:S(2)}) copy-start(f32[1024]{0:T(1024)} %param.14) | copy-start | bytes 12292
  2.1 4.5 %collective-permute-start = (f32[520,128]{1,0:T(8,128)S(1)}, f32[520,128]{1,0:T(8,128)S(1)}, u32[]{:S(2)}, u32[]{:S(2)}) collective-permute-start(f32[520,128]{1,0:T(8,128)S(1)} %get-tuple-element.56), channel_id=1, source_target_pairs={{0,4},{4,0},{8,12},{12,8},{16,20},{20,16},{24,28},{28,24},{32,36},... | collective-permute-start | bytes 798728 | tf_op jit(solution)/shard_map/ppermute | solution.py:462
  42.3 5.0 %collective-permute-start.1 = (f32[512,128]{1,0:T(8,128)S(1)}, f32[512,128]{1,0:T(8,128)S(1)}, u32[]{:S(2)}, u32[]{:S(2)}) collective-permute-start(f32[512,128]{1,0:T(8,128)S(1)} %get-tuple-element.60), channel_id=1, source_target_pairs={{0,4},{4,0},{8,12},{12,8},{16,20},{20,16},{24,28},{28,24},{32,36},... | collective-permute-start | bytes 786440 | tf_op jit(solution)/shard_map/ppermute | solution.py:473
  47.7 6.2 %collective-permute-start.4 = (f32[8,256]{1,0:T(8,128)S(1)}, f32[8,256]{1,0:T(8,128)S(1)}, u32[]{:S(2)}, u32[]{:S(2)}) collective-permute-start(f32[8,256]{1,0:T(8,128)S(1)} %get-tuple-element.65.sums0), channel_id=1, source_target_pairs={{0,3},{1,0},{2,1},{3,2},{4,7},{5,4},{6,5},{7,6},{8,11},{9,8},{10,9... | collective-permute-start | bytes 24584 | tf_op jit(solution)/shard_map/ppermute | solution.py:451
  50.4 3.7 %collective-permute-start.3 = (f32[8,256]{1,0:T(8,128)S(1)}, f32[8,256]{1,0:T(8,128)S(1)}, u32[]{:S(2)}, u32[]{:S(2)}) collective-permute-start(f32[8,256]{1,0:T(8,128)S(1)} %get-tuple-element.65.sums0), channel_id=1, source_target_pairs={{0,1},{1,2},{2,3},{3,0},{4,5},{5,6},{6,7},{7,4},{8,9},{9,10},{10,1... | collective-permute-start | bytes 24584 | tf_op jit(solution)/shard_map/ppermute | solution.py:451
  50.4 4.0 %collective-permute-start.2 = (f32[8,256]{1,0:T(8,128)S(1)}, f32[8,256]{1,0:T(8,128)S(1)}, u32[]{:S(2)}, u32[]{:S(2)}) collective-permute-start(f32[8,256]{1,0:T(8,128)S(1)} %get-tuple-element.65.sums0), channel_id=1, source_target_pairs={{0,2},{1,3},{2,0},{3,1},{4,6},{5,7},{6,4},{7,5},{8,10},{9,11},{10,... | collective-permute-start | bytes 24584 | tf_op jit(solution)/shard_map/ppermute | solution.py:451
  54.9 3.2 %collective-permute-start.5 = (f32[512,128]{1,0:T(8,128)S(1)}, f32[512,128]{1,0:T(8,128)S(1)}, u32[]{:S(2)}, u32[]{:S(2)}) collective-permute-start(f32[512,128]{1,0:T(8,128)S(1)} %get-tuple-element.77), channel_id=1, source_target_pairs={{0,4},{4,0},{8,12},{12,8},{16,20},{20,16},{24,28},{28,24},{32,36},... | collective-permute-start | bytes 786440 | tf_op jit(solution)/shard_map/ppermute | solution.py:496
  88.6 4.9 %collective-permute-start.6 = (f32[512,128]{1,0:T(8,128)S(1)}, f32[512,128]{1,0:T(8,128)S(1)}, u32[]{:S(2)}, u32[]{:S(2)}) collective-permute-start(f32[512,128]{1,0:T(8,128)S(1)} %get-tuple-element.82), channel_id=1, source_target_pairs={{0,4},{4,0},{8,12},{12,8},{16,20},{20,16},{24,28},{28,24},{32,36},... | collective-permute-start | bytes 786440 | tf_op jit(solution)/shard_map/ppermute | solution.py:508
